TPU v7x, 32 devices: a whole 2x2x4 slice. The times are simulated.
32 devices in a mesh: dom: 4 (over y, x), tile: 8 (over z, core).
Axes of the slice: x: 2, y: 2, z: 4, core: 2. Of those that a mesh axis runs over, the one named last changes fastest.
Arguments:
- atm_anom: bfloat16 [128, 80, 127, 128], P(('dom', 'tile')), may hold values from -0.25 to 0.25
- ocn_anom: bfloat16 [128, 80, 75, 128], P(('dom', 'tile')), may hold values from -0.25 to 0.25
- atm_vec: bfloat16 [128, 127, 128], P(('dom', 'tile')), may hold values from -6 to 6
- ocn_vec: bfloat16 [128, 75, 128], P(('dom', 'tile')), may hold values from -6 to 6
- atm_to_ocean: int32 [128, 128], P(('dom', 'tile')), may hold values from 0 to 16383, as said below
- sea_tiles: int32 [128], P(('dom', 'tile')), may hold values 0 or 1
- atm_class: int32 [128, 5], P(('dom', 'tile')), may hold values from 0 to 4
- ocn_class: int32 [128, 5], P(('dom', 'tile')), may hold values from 0 to 4
Outputs:
- atm_out: float32 [128, 127, 128], P(('dom', 'tile'))
- ocn_out: float32 [128, 75, 128], P(('dom', 'tile'))
Inputs may be any that keep to these rules, and one draw needn't show every extreme that they name: atm_to_ocean is one to one onto all 16384 ocean columns; the atmosphere columns held by the r-th device along dom+tile (tiles r * 4 to r * 4 + 3) are paired exactly with the ocean columns whose column index c satisfies c // (128 / number of devices) = r.
All inputs are finite; a program needn't handle non-finite values. No bound on the sum of `sea_tiles` on one device may be relied on, other than what follows from the above.
Results may differ from a plain program's by a relative error of at most 0.0029.
Values may be sent and summed in bfloat16 or wider, within the bound.
No kernel may reach another device: no remote copies, remote signals or barrier semaphores. Data moves between devices by JAX's collectives and lax.ppermute only.
A program may use at most 64 MiB of HBM per device.

v0:
```python
import jax
import jax.numpy as jnp
from jax import lax
from jax.sharding import PartitionSpec as P

KA = 16
KO = 16
HALO = 2


COUPLING = 8.0
ATM_SPREAD = 12.0
OCN_SPREAD = 8.0
CLASS_TABLE = (1.0, 0.7, 0.45, 0.25, 0.0)


def padded_2(block, sides, width):
    for axis, dim in sides:
        count = lax.axis_size(axis)
        forward = [(i, i + 1) for i in range(count - 1)]
        forward.append((count - 1, 0))
        backward = [(target, source) for source, target in forward]
        low = lax.ppermute(
            lax.slice_in_dim(block, block.shape[dim] - width, None, axis=dim), axis, forward
        )
        high = lax.ppermute(lax.slice_in_dim(block, 0, width, axis=dim), axis, backward)
        block = jnp.concatenate([low, block, high], axis=dim)
    return block


def level_taper(level_count, spread):
    position = jnp.arange(level_count, dtype=jnp.float32)
    scaled = (position[:, None] - position[None, :]) / spread
    return jnp.exp(-0.5 * scaled * scaled)


def class_weights(classes):
    class_table = jnp.array(CLASS_TABLE, jnp.float32)
    matches = classes[..., None] == jnp.arange(len(CLASS_TABLE), dtype=jnp.int32)
    return jnp.sum(jnp.where(matches, class_table, 0.0), axis=-1)


def spread_tiles(padded, classes, tile_count):
    weights = class_weights(classes)
    summed = jnp.zeros((tile_count,) + padded.shape[1:], jnp.float32)
    for offset in range(2 * HALO + 1):
        summed = summed + weights[:, offset, None, None] * padded[offset : offset + tile_count]
    return summed


def vertical(spread, tapering):
    return jnp.einsum("tmk,lk->tml", spread, tapering, precision=lax.Precision.HIGHEST).astype(
        jnp.bfloat16
    )


def local(atm_anom, ocn_anom, atm_vec, ocn_vec, atm_to_ocean, sea_tiles, atm_class, ocn_class):
    tile_count, members, atm_levels, columns = atm_anom.shape
    ocn_levels = ocn_anom.shape[2]
    device_count = lax.axis_size("dom") * lax.axis_size("tile")
    per_peer = columns // device_count
    flat_width = tile_count * columns
    surface_start = atm_levels - KA
    rise_position = jnp.arange(KA, dtype=jnp.float32)
    rise_weights = jnp.exp(-2.0 * (KA - 1 - rise_position) / KA)
    fall_position = jnp.arange(KO, dtype=jnp.float32)
    fall_weights = jnp.exp(-2.0 * fall_position / KO)
    sea_flags = sea_tiles.astype(jnp.float32)
    target = atm_to_ocean.reshape(flat_width)
    ocean_tile = target // columns
    ocean_column = target % columns
    slot_index = (
        ocean_tile % tile_count * columns
        + ocean_tile // tile_count * per_peer
        + ocean_column % per_peer
    )
    slot_source = (
        jnp.zeros_like(slot_index).at[slot_index].set(jnp.arange(flat_width, dtype=jnp.int32))
    )
    atm_surface = atm_anom[:, :, surface_start:, :]
    ocn_top = ocn_anom[:, :, :KO, :]
    atm_coeff = jnp.einsum("tmlc,tlc->tml", atm_anom, atm_vec, preferred_element_type=jnp.float32)
    ocn_coeff = (
        jnp.einsum("tmlc,tlc->tml", ocn_anom, ocn_vec, preferred_element_type=jnp.float32)
        * sea_flags[:, None, None]
    )
    joined = jnp.concatenate([atm_coeff, ocn_coeff], axis=2)
    padded = padded_2(joined, (("tile", 0),), HALO)
    atm_weighted = atm_vec[:, surface_start:, :].astype(jnp.float32) * rise_weights[None, :, None]
    atm_proj = jnp.einsum("tmsc,tsc->mtc", atm_surface.astype(jnp.float32), atm_weighted).astype(
        jnp.bfloat16
    )
    outgoing = jnp.take(atm_proj.reshape(members, flat_width), slot_source, axis=1).reshape(
        members, tile_count, columns
    )
    ocean_proj = lax.all_to_all(outgoing, ("dom", "tile"), split_axis=2, concat_axis=2, tiled=True)
    ocn_weighted = (
        ocn_vec[:, :KO, :].astype(jnp.float32)
        * fall_weights[None, :, None]
        * sea_flags[:, None, None]
    )
    ocn_proj = jnp.einsum("tmoc,toc->mtc", ocn_top.astype(jnp.float32), ocn_weighted).astype(
        jnp.bfloat16
    )
    returned = lax.all_to_all(ocn_proj, ("dom", "tile"), split_axis=2, concat_axis=2, tiled=True)
    atm_pair = jnp.take(returned.reshape(members, flat_width), slot_index, axis=1).reshape(
        members, tile_count, columns
    )
    ocean_proj, atm_pair = (ocean_proj, atm_pair)
    atm_spread = spread_tiles(padded[:, :, :atm_levels], atm_class, tile_count)
    ocn_spread = spread_tiles(padded[:, :, atm_levels:], ocn_class, tile_count)
    atm_vertical = vertical(atm_spread, level_taper(atm_levels, ATM_SPREAD))
    ocn_vertical = vertical(ocn_spread, level_taper(ocn_levels, OCN_SPREAD))
    atm_out = jnp.einsum(
        "tmlc,tml->tlc", atm_anom, atm_vertical, preferred_element_type=jnp.float32
    )
    atm_cross = (
        jnp.einsum("tmsc,mtc->tsc", atm_surface, atm_pair, preferred_element_type=jnp.float32)
        * (COUPLING * rise_weights)[None, :, None]
    )
    atm_out = atm_out.at[:, surface_start:, :].add(atm_cross)
    ocean_paired = jnp.transpose(ocean_proj, (1, 0, 2))

    def second_pass(anomaly, vertical_coeff, paired):
        intra_part = jnp.einsum(
            "mlc,ml->lc", anomaly, vertical_coeff, preferred_element_type=jnp.float32
        )
        cross_part = (
            jnp.einsum("moc,mc->oc", anomaly[:, :KO], paired, preferred_element_type=jnp.float32)
            * (COUPLING * fall_weights)[:, None]
        )
        return intra_part.at[:KO].add(cross_part)

    ocn_out = jax.vmap(second_pass)(ocn_anom, ocn_vertical, ocean_paired) * sea_flags[:, None, None]
    return (atm_out, ocn_out)


def solution(mesh):
    in_specs = (
        P(("dom", "tile"), None, None, None),
        P(("dom", "tile"), None, None, None),
        P(("dom", "tile"), None, None),
        P(("dom", "tile"), None, None),
        P(("dom", "tile"), None),
        P(("dom", "tile")),
        P(("dom", "tile"), None),
        P(("dom", "tile"), None),
    )
    out_specs = (P(("dom", "tile"), None, None), P(("dom", "tile"), None, None))
    return jax.shard_map(local, mesh=mesh, in_specs=in_specs, out_specs=out_specs, check_vma=False)
```

profile of v0, /device:TPU:0, one launch (start us, length us, event | category | flops | bytes accessed | tf_op | source)
XLA Modules:
  0.0 64.0 jit_solution(15735082124736404035)
XLA Ops:
  0.6 6.1 %fusion.22 = f32[4,75,1,80]{3,2,1,0:T(1,128)S(1)} fusion(bf16[4,80,75,128]{3,1,2,0:T(8,128)(2,1)} %param.17, bf16[4,75,128,1]{2,0,1,3:T(4,128)(2,1)} %bitcast.119), kind=kOutput, calls=%fused_computation.41 | convolution fusion | flops 6144000 | bytes 6316800 | tf_op jit(solution)/shard_map/tmlc,tlc->tml/dot_general | solution.py:84
  7.0 8.0 %fusion.2 = f32[4,127,1,80]{3,2,1,0:T(1,128)S(1)} fusion(bf16[4,80,127,128]{3,1,2,0:T(8,128)(2,1)} %param.16, bf16[4,127,128,1]{2,0,1,3:T(4,128)(2,1)S(1)} %bitcast.116), kind=kOutput, calls=%fused_computation.16 | convolution fusion | flops 10403840 | bytes 10696448 | tf_op jit(solution)/shard_map/tmlc,tlc->tml/dot_general | solution.py:82
  15.4 0.5 collective-permute-start
  15.9 4.1 %collective-permute-start.1 = (f32[2,80,202]{2,1,0:T(8,128)S(1)}, f32[2,80,202]{2,1,0:T(8,128)S(1)}, u32[]{:S(2)}, u32[]{:S(2)}) collective-permute-start(f32[2,80,202]{2,1,0:T(8,128)S(1)} %get-tuple-element.34), channel_id=1, source_target_pairs={{1,0},{2,1},{3,2},{4,3},{5,4},{6,5},{7,6},{0,7},{9,8},{10,9},{11,1... | collective-permute-start | bytes 387848 | tf_op jit(solution)/shard_map/ppermute | solution.py:26
  20.0 0.8 %multiply_bitcast_fusion.1 = f32[4,128,16]{1,0,2:T(4,128)S(1)} fusion(f32[4]{0:T(128)S(1)} %convert_element_type.29, f32[16]{0:T(128)S(1)} %multiply_exponential_fusion.1, bf16[4,75,128]{2,0,1:T(4,128)(2,1)} %param.19), kind=kLoop, calls=%fused_computation.80 | loop fusion | flops 24576 | bytes 49232
  20.8 1.6 %multiply_reduce_fusion.3 = bf16[4,128,80]{1,2,0:T(8,128)(2,1)S(1)} fusion(f32[4,128,16]{1,2,0:T(8,128)S(1)} %copy.58, bf16[4,80,75,128]{3,1,2,0:T(8,128)(2,1)} %param.17), kind=kLoop, calls=%fused_computation.6 | loop fusion | flops 1925120 | bytes 1425408
  22.4 0.8 %copy.66 = bf16[4,128,80]{2,0,1:T(4,128)(2,1)} copy(bf16[4,128,80]{1,2,0:T(8,128)(2,1)S(1)} %multiply_reduce_fusion.3) | data formatting | bytes 163840
  23.2 4.5 %all-to-all-start = ((bf16[80,4,128]{0,1,2:T(4,128)(2,1)}), bf16[80,4,128]{0,1,2:T(4,128)(2,1)S(1)}, u32[]{:S(2)}, u32[]{:S(2)}) async-start(bf16[80,4,128]{0,1,2:T(4,128)(2,1)} %bitcast.24), calls=%async_computation | async-start | bytes 262144 | tf_op jit(solution)/shard_map/all_to_all | solution.py:105
  27.9 2.4 %scatter_custom_fusion = s32[512]{0:T(512)S(1)} fusion(s32[512]{0:T(512)S(1)} %bitcast.122, s32[512]{0:T(512)S(1)} %iota.42, s32[]{:T(128)} %constant.143.clone.1), kind=kCustom, calls=%fused_computation.138 | custom fusion | bytes 2052 | tf_op jit(solution)/shard_map/scatter | solution.py:78
  30.6 1.6 %multiply_reduce_fusion.1 = bf16[4,128,80]{1,2,0:T(8,128)(2,1)S(1)} fusion(f32[4,128,16]{1,2,0:T(8,128)S(1)} %copy.60, bf16[4,80,127,128]{3,1,2,0:T(8,128)(2,1)} %param.16), kind=kLoop, calls=%fused_computation.4 | loop fusion | flops 1925120 | bytes 1425408
  32.6 1.3 %gather_fusion.1 = bf16[512,80]{1,0:T(8,128)(2,1)S(1)} fusion(bf16[80,512]{0,1:T(8,128)(2,1)S(1)} %bitcast.112, s32[1024]{0:T(1024)S(1)} %pad_clamp_fusion), kind=kCustom, calls=%fused_computation.1.clone | custom fusion | bytes 165888 | tf_op jit(solution)/shard_map/jit(_take)/gather | solution.py:93
  34.1 0.8 %copy.17 = bf16[80,4,128]{0,1,2:T(4,128)(2,1)} copy(bf16[80,4,128]{0,2,1:T(8,128)(2,1)S(1)} %bitcast.117) | data formatting | bytes 163840 | tf_op jit(solution)/shard_map/reshape | solution.py:93
  34.9 0.2 maximum_maximum_fusion
  35.1 0.4 fusion
  35.7 5.5 %fusion.76 = f32[4,127,1,128]{3,2,1,0:T(1,128)S(1)} fusion(bf16[4,80,127,1]{1,3,2,0:T(2,128)(2,1)S(1)} %copy.22, bf16[4,80,127,128]{3,1,2,0:T(8,128)(2,1)} %param.16), kind=kOutput, calls=%fused_computation.159 | convolution fusion | flops 10403840 | bytes 10745216 | tf_op jit(solution)/shard_map/tmlc,tml->tlc/dot_general | solution.py:114
  41.2 0.5 fusion.1
  41.8 4.4 %fusion.77 = f32[4,75,1,128]{3,2,1,0:T(1,128)S(1)} fusion(bf16[4,80,75,1]{1,3,2,0:T(2,128)(2,1)S(1)} %copy.40, bf16[4,80,75,128]{3,1,2,0:T(8,128)(2,1)} %param.17), kind=kOutput, calls=%fused_computation.160 | convolution fusion | flops 6144000 | bytes 6345600 | tf_op jit(solution)/shard_map/vmap(mlc,ml->lc)/dot_general | solution.py:125
  46.4 5.8 %all-to-all-start.1 = ((bf16[80,4,128]{0,1,2:T(4,128)(2,1)}), bf16[80,4,128]{0,1,2:T(4,128)(2,1)S(1)}, u32[]{:S(2)}, u32[]{:S(2)}) async-start(bf16[80,4,128]{0,1,2:T(4,128)(2,1)} %copy.17), calls=%async_computation.1 | async-start | bytes 262144 | tf_op jit(solution)/shard_map/all_to_all | solution.py:96
  52.3 1.3 %gather_fusion = bf16[512,80]{1,0:T(8,128)(2,1)S(1)} fusion(bf16[80,512]{0,1:T(8,128)(2,1)S(1)} %bitcast.111, s32[1024]{0:T(1024)S(1)} %pad_clamp_fusion.1), kind=kCustom, calls=%fused_computation.clone | custom fusion | bytes 165888 | tf_op jit(solution)/shard_map/jit(_take)/gather | solution.py:106
  53.9 1.7 %multiply_reduce_fusion.2 = f32[4,128,16]{1,2,0:T(8,128)S(1)} fusion(f32[4,128,80]{1,2,0:T(8,128)S(1)} %copy.59, bf16[4,80,127,128]{3,1,2,0:T(8,128)(2,1)} %param.16), kind=kLoop, calls=%fused_computation.5 | loop fusion | flops 1957888 | bytes 1507328
  55.6 4.9 %all-to-all-done.1 = bf16[80,4,128]{0,1,2:T(4,128)(2,1)S(1)} async-done(((bf16[80,4,128]{0,1,2:T(4,128)(2,1)}), bf16[80,4,128]{0,1,2:T(4,128)(2,1)S(1)}, u32[]{:S(2)}, u32[]{:S(2)}) %all-to-all-start.1) | async-done | bytes 81952 | tf_op jit(solution)/shard_map/all_to_all | solution.py:96
  60.6 1.7 %multiply_reduce_fusion = f32[4,128,16]{1,2,0:T(8,128)S(1)} fusion(f32[4,128,80]{1,2,0:T(8,128)S(1)} %copy.61, bf16[4,80,75,128]{3,1,2,0:T(8,128)(2,1)} %param.17), kind=kLoop, calls=%fused_computation.3 | loop fusion | flops 1957888 | bytes 1507328
  62.4 0.8 %broadcast_multiply_fusion = f32[4,75,128]{2,0,1:T(4,128)} fusion(f32[4,75,128]{2,0,1:T(4,128)S(1)} %fusion.50, f32[4]{0:T(128)S(1)} %convert_element_type.29), kind=kLoop, calls=%fused_computation.56 | loop fusion | flops 38400 | bytes 307216 | tf_op jit(solution)/shard_map/mul | solution.py:134
  63.3 0.7 %copy-done.1 = f32[4,127,128]{2,0,1:T(4,128)} copy-done((f32[4,127,128]{2,0,1:T(4,128)}, f32[4,127,128]{2,0,1:T(4,128)S(1)}, u32[]{:S(2)}) %copy-start.1) | copy-done | bytes 260120
  (52 shorter events, 2.5 us)
Async XLA Ops:
  0.6 6.2 %copy-start.6 = (s32[4]{0:T(128)S(1)}, s32[4]{0:T(128)}, u32[]{:S(2)}) copy-start(s32[4]{0:T(128)} %param.21) | copy-start | bytes 52
  0.6 6.3 %copy-start = (bf16[4,127,128]{2,0,1:T(4,128)(2,1)S(1)}, bf16[4,127,128]{2,0,1:T(4,128)(2,1)}, u32[]{:S(2)}) copy-start(bf16[4,127,128]{2,0,1:T(4,128)(2,1)} %param.18) | copy-start | bytes 390148
  6.9 20.9 %copy-start.2 = (s32[4,128]{1,0:T(4,128)S(1)}, s32[4,128]{1,0:T(4,128)}, u32[]{:S(2)}) copy-start(s32[4,128]{1,0:T(4,128)} %param.20) | copy-start | bytes 6148
  6.9 23.4 %copy-start.3 = (s32[4,5]{1,0:T(4,128)S(1)}, s32[4,5]{1,0:T(4,128)}, u32[]{:S(2)}) copy-start(s32[4,5]{1,0:T(4,128)} %param.23) | copy-start | bytes 244
  6.9 23.5 %copy-start.4 = (s32[4,5]{1,0:T(4,128)S(1)}, s32[4,5]{1,0:T(4,128)}, u32[]{:S(2)}) copy-start(s32[4,5]{1,0:T(4,128)} %param.22) | copy-start | bytes 244
  6.9 25.5 %copy-start.5 = (f32[5]{0:T(128)S(1)}, f32[5]{0:T(128)}, u32[]{:S(2)}) copy-start(f32[5]{0:T(128)} %constant.157.clone) | copy-start | bytes 64
  15.4 19.5 %collective-permute-start = (f32[2,80,202]{2,1,0:T(8,128)S(1)}, f32[2,80,202]{2,1,0:T(8,128)S(1)}, u32[]{:S(2)}, u32[]{:S(2)}) collective-permute-start(f32[2,80,202]{2,1,0:T(8,128)S(1)} %get-tuple-element.33), channel_id=1, source_target_pairs={{0,1},{1,2},{2,3},{3,4},{4,5},{5,6},{6,7},{7,0},{8,9},{9,10},{10,1... | collective-permute-start | bytes 387848 | tf_op jit(solution)/shard_map/ppermute | solution.py:23
  15.9 19.0 %collective-permute-start.1 = (f32[2,80,202]{2,1,0:T(8,128)S(1)}, f32[2,80,202]{2,1,0:T(8,128)S(1)}, u32[]{:S(2)}, u32[]{:S(2)}) collective-permute-start(f32[2,80,202]{2,1,0:T(8,128)S(1)} %get-tuple-element.34), channel_id=1, source_target_pairs={{1,0},{2,1},{3,2},{4,3},{5,4},{6,5},{7,6},{0,7},{9,8},{10,9},{11,1... | collective-permute-start | bytes 387848 | tf_op jit(solution)/shard_map/ppermute | solution.py:26
  23.2 23.2 %all-to-all-start = ((bf16[80,4,128]{0,1,2:T(4,128)(2,1)}), bf16[80,4,128]{0,1,2:T(4,128)(2,1)S(1)}, u32[]{:S(2)}, u32[]{:S(2)}) async-start(bf16[80,4,128]{0,1,2:T(4,128)(2,1)} %bitcast.24), calls=%async_computation | async-start | bytes 262144 | tf_op jit(solution)/shard_map/all_to_all | solution.py:105
  46.4 14.0 %all-to-all-start.1 = ((bf16[80,4,128]{0,1,2:T(4,128)(2,1)}), bf16[80,4,128]{0,1,2:T(4,128)(2,1)S(1)}, u32[]{:S(2)}, u32[]{:S(2)}) async-start(bf16[80,4,128]{0,1,2:T(4,128)(2,1)} %copy.17), calls=%async_computation.1 | async-start | bytes 262144 | tf_op jit(solution)/shard_map/all_to_all | solution.py:96
  63.3 0.7 %copy-start.1 = (f32[4,127,128]{2,0,1:T(4,128)}, f32[4,127,128]{2,0,1:T(4,128)S(1)}, u32[]{:S(2)}) copy-start(f32[4,127,128]{2,0,1:T(4,128)S(1)} %fusion.51) | copy-start | bytes 780292
where the time goes:
time: 64.4 us; the launch traced here: 64 us
  matrix products  24.9 us (39%)
  starting transfers between devices  14.9 us (23%)
  other arithmetic  9.53 us (15%)
  local copies, waits for them, and re-layouts  8.76 us (14%)
  waiting for transfers between devices  4.86 us (8%)
  between operations  0.99 us (2%)
    dot_general x1, matrix products, local(): jnp.einsum('tmlc,tlc->tml', atm_anom, atm_vec, preferred_element_type=jnp...  8.04 us
    unnamed x7, other arithmetic  7.52 us
    dot_general x1, matrix products, local(): jnp.einsum('tmlc,tlc->tml', ocn_anom, ocn_vec, preferred_element_type=jnp...  6.07 us
    all_to_all x1, starting transfers between devices, local(): lax.all_to_all(outgoing, ('dom', 'tile'), split_axis=2, concat_axis=2, ti...  5.84 us
    dot_general x1, matrix products, local(): jnp.einsum('tmlc,tml->tlc', atm_anom, atm_vertical, preferred_element_typ...  5.49 us
    all_to_all x1, waiting for transfers between devices, local(): lax.all_to_all(outgoing, ('dom', 'tile'), split_axis=2, concat_axis=2, ti...  4.85 us
    all_to_all x1, starting transfers between devices, local(): lax.all_to_all(ocn_proj, ('dom', 'tile'), split_axis=2, concat_axis=2, ti...  4.49 us
    dot_general x1, matrix products, second_pass(): jnp.einsum('mlc,ml->lc', anomaly, vertical_coeff, preferred_element_type=...  4.43 us
  transfers between devices with their start and end apart: 4, of which 1 were waited for; matrix products, arithmetic and copies ran while one was open for 39% of the time, Pallas kernels for 0%

commit v1 on v0

v1 whole, which is shorter than its diff:
```python
import functools
import math

import jax
import jax.numpy as jnp
from jax import lax
from jax.experimental import pallas as pl
from jax.experimental.pallas import tpu as pltpu
from jax.sharding import PartitionSpec as P

KA = 16
KO = 16
HALO = 2

COUPLING = 8.0
ATM_SPREAD = 12.0
OCN_SPREAD = 8.0
CLASS_TABLE = (1.0, 0.7, 0.45, 0.25, 0.0)

BF16 = jnp.bfloat16
F32 = jnp.float32
MIB = 1 << 20
NT = (((1,), (1,)), ((), ()))
TN = (((0,), (0,)), ((), ()))
VMEM_SPEC = pl.BlockSpec(memory_space=pltpu.VMEM)
SMEM_SPEC = pl.BlockSpec(memory_space=pltpu.SMEM)
ANY_SPEC = pl.BlockSpec(memory_space=pl.ANY)

RISE = [math.exp(-2.0 * (KA - 1 - s) / KA) for s in range(KA)]
FALL = [math.exp(-2.0 * o / KO) for o in range(KO)]


def slot_rows(index, columns, tiles, per_peer):
    tile, column = index // columns, index % columns
    return (tile // tiles) * (tiles * per_peer) + (tile % tiles) * per_peer + column % per_peer


def one_hot(rows, width):
    position = lax.broadcasted_iota(jnp.int32, (width, rows.shape[1]), 0)
    return jnp.where(position == rows, 1.0, 0.0).astype(BF16)


def atm_slots(pairing_ref, columns, tiles, per_peer):
    index = jnp.concatenate([pairing_ref[t : t + 1, :] for t in range(tiles)], axis=1)
    return one_hot(slot_rows(index, columns, tiles, per_peer), tiles * columns)


def ocn_slots(columns, tiles, per_peer):
    place = lax.broadcasted_iota(jnp.int32, (1, tiles * columns), 1)
    tile, column = place // columns, place % columns
    rows = (column // per_peer) * (tiles * per_peer) + tile * per_peer + column % per_peer
    return one_hot(rows, tiles * columns)


def first_kernel(
    per_peer,
    sea_ref,
    pairing_ref,
    atm_vec_ref,
    ocn_vec_ref,
    atm_hbm,
    ocn_hbm,
    atm_ref,
    ocn_ref,
    low_ref,
    high_ref,
    atm_send_ref,
    ocn_send_ref,
    vec_ref,
    weight_ref,
    sems,
):
    tiles, atm_levels, members, columns = atm_hbm.shape
    ocn_levels = ocn_hbm.shape[1]
    copies = {}
    for t in range(tiles):
        copies["a", t] = pltpu.make_async_copy(atm_hbm.at[t], atm_ref.at[t], sems.at[0, t])
        copies["o", t] = pltpu.make_async_copy(ocn_hbm.at[t], ocn_ref.at[t], sems.at[1, t])
    for t in range(tiles):
        copies["a", t].start()
    for t in range(tiles):
        copies["o", t].start()

    lane = lax.broadcasted_iota(jnp.int32, (members, columns), 1)
    weight_ref[...] = jnp.zeros_like(weight_ref)

    def load_vec(source_ref, t, levels):
        vec_ref[...] = jnp.zeros_like(vec_ref)
        vec_ref[:levels] = source_ref[:, t, :].astype(F32)

    def coefficients(ref, t, levels):
        half = (levels + 1) // 2
        second = levels - half
        vec_t = vec_ref[...].T.astype(BF16)
        weight_ref[:columns, :columns] = vec_t
        weight_ref[columns:, columns:] = vec_t
        rows = jnp.concatenate(
            [
                ref[t, 0:half].reshape(half * members, columns),
                ref[t, second:levels].reshape(half * members, columns),
            ],
            axis=1,
        )
        product = jnp.dot(rows, weight_ref[...], preferred_element_type=F32)
        total = jnp.zeros((members, columns), F32)
        for j in range(half):
            part = product[j * members : (j + 1) * members]
            total = jnp.where(lane == j, part[:, :columns], total)
            total = jnp.where(lane == second + j, part[:, columns:], total)
        return total

    def projection(ref, t, start, weights):
        total = jnp.zeros((members, columns), F32)
        for s, weight in enumerate(weights):
            row = vec_ref[start + s : start + s + 1, :] * weight
            total = total + ref[t, start + s].astype(F32) * row
        return total

    def store(t, which, value):
        if t < tiles // 2:
            high_ref[t, which] = value
        else:
            low_ref[t - tiles // 2, which] = value

    atm_proj = []
    for t in range(tiles):
        load_vec(atm_vec_ref, t, atm_levels)
        copies["a", t].wait()
        store(t, 0, coefficients(atm_ref, t, atm_levels))
        atm_proj.append(projection(atm_ref, t, atm_levels - KA, RISE).astype(BF16))
    atm_send_ref[...] = lax.dot_general(
        atm_slots(pairing_ref, columns, tiles, per_peer),
        jnp.concatenate(atm_proj, axis=1),
        NT,
        preferred_element_type=F32,
    ).astype(BF16)
    ocn_proj = []
    for t in range(tiles):
        load_vec(ocn_vec_ref, t, ocn_levels)
        sea = sea_ref[t].astype(F32)
        copies["o", t].wait()
        store(t, 1, coefficients(ocn_ref, t, ocn_levels) * sea)
        ocn_proj.append((projection(ocn_ref, t, 0, FALL) * sea).astype(BF16))
    ocn_send_ref[...] = lax.dot_general(
        ocn_slots(columns, tiles, per_peer),
        jnp.concatenate(ocn_proj, axis=1),
        NT,
        preferred_element_type=F32,
    ).astype(BF16)


def second_kernel(
    sea_ref,
    atm_class_ref,
    ocn_class_ref,
    atm_ref,
    ocn_ref,
    low_ref,
    own_low_ref,
    own_high_ref,
    high_ref,
    atm_out_ref,
    ocn_out_ref,
    vert_ref,
):
    tiles, atm_levels, members, columns = atm_ref.shape
    ocn_levels = ocn_ref.shape[1]
    padded = [(low_ref, 0), (low_ref, 1), (own_low_ref, 0), (own_low_ref, 1)]
    padded += [(own_high_ref, 0), (own_high_ref, 1), (high_ref, 0), (high_ref, 1)]
    group = 16
    sub = lax.broadcasted_iota(jnp.int32, (group, columns), 0)
    row = lax.broadcasted_iota(jnp.int32, (columns, columns), 0)
    col = lax.broadcasted_iota(jnp.int32, (columns, columns), 1)

    def class_weight(number):
        weight = jnp.float32(0.0)
        for value, factor in enumerate(CLASS_TABLE):
            weight = jnp.where(number == value, jnp.float32(factor), weight)
        return weight

    def taper(spread):
        scaled = (row - col).astype(F32) * (1.0 / spread)
        return jnp.exp(-0.5 * scaled * scaled)

    for which, (ref, out_ref, class_ref, levels, width) in enumerate(
        [
            (atm_ref, atm_out_ref, atm_class_ref, atm_levels, ATM_SPREAD),
            (ocn_ref, ocn_out_ref, ocn_class_ref, ocn_levels, OCN_SPREAD),
        ]
    ):
        tapering = taper(width)
        for t in range(tiles):
            spread = jnp.zeros((members, columns), F32)
            for offset in range(2 * HALO + 1):
                source, place = padded[t + offset]
                spread = spread + class_weight(class_ref[t, offset]) * source[place, which]
            vert_ref[t] = lax.dot_general(
                tapering, spread, NT, precision=lax.Precision.HIGHEST, preferred_element_type=F32
            ).astype(BF16)

        @pl.loop(0, tiles)
        def _(t):
            sea = sea_ref[t].astype(F32)
            for start in range(0, levels, group):
                count = min(group, levels - start)
                right = jnp.concatenate([ref[t, start + j] for j in range(count)], axis=1)
                product = jnp.dot(
                    vert_ref[t, start : start + group, :], right, preferred_element_type=F32
                )
                total = product[:, :columns]
                for j in range(1, count):
                    total = jnp.where(sub == j, product[:, j * columns : (j + 1) * columns], total)
                if which == 1:
                    total = total * sea
                out_ref[start : start + count, t, :] = total[:count]


def cross_kernel(
    per_peer,
    sea_ref,
    pairing_ref,
    atm_recv_ref,
    ocn_recv_ref,
    atm_top_hbm,
    ocn_top_hbm,
    atm_in,
    ocn_in,
    atm_out,
    ocn_out,
    atm_top,
    ocn_top,
    atm_rows,
    ocn_rows,
    sems,
):
    tiles, atm_levels, members, columns = atm_top_hbm.shape
    start = atm_levels - KA
    loads = [
        pltpu.make_async_copy(atm_in.at[pl.ds(start, KA)], atm_rows, sems.at[0]),
        pltpu.make_async_copy(ocn_in.at[pl.ds(0, KO)], ocn_rows, sems.at[1]),
        pltpu.make_async_copy(atm_top_hbm.at[:, pl.ds(start, KA)], atm_top, sems.at[2]),
        pltpu.make_async_copy(ocn_top_hbm.at[:, pl.ds(0, KO)], ocn_top, sems.at[3]),
    ]
    for load in loads:
        load.start()
    atm_pair = lax.dot_general(
        ocn_recv_ref[...],
        atm_slots(pairing_ref, columns, tiles, per_peer),
        TN,
        preferred_element_type=F32,
    )
    ocn_pair = lax.dot_general(
        atm_recv_ref[...],
        ocn_slots(columns, tiles, per_peer),
        TN,
        preferred_element_type=F32,
    )
    for load in loads:
        load.wait()

    def add(top, rows, pair, weights, scale):
        for t in range(tiles):
            paired = pair[:, t * columns : (t + 1) * columns]
            sums = [
                jnp.sum(top[t, s].astype(F32) * paired, axis=0, keepdims=True) * (COUPLING * weight)
                for s, weight in enumerate(weights)
            ]
            rows[:, t, :] = rows[:, t, :] + jnp.concatenate(sums, axis=0) * scale(t)

    add(atm_top, atm_rows, atm_pair, RISE, lambda t: jnp.float32(1.0))
    add(ocn_top, ocn_rows, ocn_pair, FALL, lambda t: sea_ref[t].astype(F32))
    stores = [
        pltpu.make_async_copy(atm_rows, atm_out.at[pl.ds(start, KA)], sems.at[0]),
        pltpu.make_async_copy(ocn_rows, ocn_out.at[pl.ds(0, KO)], sems.at[1]),
    ]
    for store in stores:
        store.start()
    for store in stores:
        store.wait()


def local(atm_anom, ocn_anom, atm_vec, ocn_vec, atm_to_ocean, sea_tiles, atm_class, ocn_class):
    tiles, members, atm_levels, columns = atm_anom.shape
    ocn_levels = ocn_anom.shape[2]
    axes = ("dom", "tile")
    devices = lax.axis_size("dom") * lax.axis_size("tile")
    per_peer = columns // devices
    peer_rows = tiles * per_peer
    slots = tiles * columns

    by_level = (0, 2, 1, 3)
    atm = jnp.transpose(atm_anom, by_level)
    ocn = jnp.transpose(ocn_anom, by_level)
    atm_rows = jnp.transpose(atm_vec, (1, 0, 2))
    ocn_rows = jnp.transpose(ocn_vec, (1, 0, 2))

    edge = jax.ShapeDtypeStruct((tiles // 2, 2, members, columns), F32)
    send = jax.ShapeDtypeStruct((slots, members), BF16)
    atm_v, ocn_v, own_high, own_low, atm_send, ocn_send = pl.pallas_call(
        functools.partial(first_kernel, per_peer),
        out_shape=[
            pltpu.VMEM(atm.shape, BF16),
            pltpu.VMEM(ocn.shape, BF16),
            edge,
            edge,
            send,
            send,
        ],
        in_specs=[SMEM_SPEC, VMEM_SPEC, VMEM_SPEC, VMEM_SPEC, ANY_SPEC, ANY_SPEC],
        out_specs=[VMEM_SPEC] * 6,
        scratch_shapes=[
            pltpu.VMEM((columns, columns), F32),
            pltpu.VMEM((2 * columns, 2 * columns), BF16),
            pltpu.SemaphoreType.DMA((2, tiles)),
        ],
        compiler_params=pltpu.CompilerParams(vmem_limit_bytes=44 * MIB),
        name="first_pass",
    )(sea_tiles, atm_to_ocean, atm_rows, ocn_rows, atm, ocn)

    count = lax.axis_size("tile")
    forward = [(i, (i + 1) % count) for i in range(count)]
    backward = [(target, source) for source, target in forward]
    low = lax.ppermute(own_high, "tile", forward)
    high = lax.ppermute(own_low, "tile", backward)

    outgoing = jnp.concatenate(
        [
            atm_send.reshape(devices, peer_rows, members),
            ocn_send.reshape(devices, peer_rows, members),
        ],
        axis=1,
    )
    incoming = lax.all_to_all(outgoing, axes, split_axis=0, concat_axis=0, tiled=True)
    atm_recv = incoming[:, :peer_rows].reshape(slots, members)
    ocn_recv = incoming[:, peer_rows:].reshape(slots, members)

    elements = tiles * members * columns * (atm_levels + ocn_levels)
    outs = [
        jax.ShapeDtypeStruct((atm_levels, tiles, columns), F32),
        jax.ShapeDtypeStruct((ocn_levels, tiles, columns), F32),
    ]
    atm_out, ocn_out = pl.pallas_call(
        second_kernel,
        out_shape=outs,
        in_specs=[SMEM_SPEC] * 3 + [VMEM_SPEC] * 6,
        out_specs=[VMEM_SPEC] * 2,
        scratch_shapes=[pltpu.VMEM((tiles, columns, members), BF16)],
        compiler_params=pltpu.CompilerParams(vmem_limit_bytes=24 * MIB),
        cost_estimate=pl.CostEstimate(
            flops=2 * 16 * elements, bytes_accessed=2 * elements, transcendentals=0
        ),
        name="second_pass",
    )(sea_tiles, atm_class, ocn_class, atm_v, ocn_v, low, own_low, own_high, high)

    atm_out, ocn_out = pl.pallas_call(
        functools.partial(cross_kernel, per_peer),
        out_shape=outs,
        in_specs=[SMEM_SPEC] + [VMEM_SPEC] * 3 + [ANY_SPEC] * 4,
        out_specs=[ANY_SPEC] * 2,
        input_output_aliases={6: 0, 7: 1},
        scratch_shapes=[
            pltpu.VMEM((tiles, KA, members, columns), BF16),
            pltpu.VMEM((tiles, KO, members, columns), BF16),
            pltpu.VMEM((KA, tiles, columns), F32),
            pltpu.VMEM((KO, tiles, columns), F32),
            pltpu.SemaphoreType.DMA((4,)),
        ],
        compiler_params=pltpu.CompilerParams(vmem_limit_bytes=24 * MIB),
        name="surface_cross",
    )(sea_tiles, atm_to_ocean, atm_recv, ocn_recv, atm, ocn, atm_out, ocn_out)
    return jnp.transpose(atm_out, (1, 0, 2)), jnp.transpose(ocn_out, (1, 0, 2))


def solution(mesh):
    in_specs = (
        P(("dom", "tile"), None, None, None),
        P(("dom", "tile"), None, None, None),
        P(("dom", "tile"), None, None),
        P(("dom", "tile"), None, None),
        P(("dom", "tile"), None),
        P(("dom", "tile")),
        P(("dom", "tile"), None),
        P(("dom", "tile"), None),
    )
    out_specs = (P(("dom", "tile"), None, None), P(("dom", "tile"), None, None))
    return jax.shard_map(local, mesh=mesh, in_specs=in_specs, out_specs=out_specs, check_vma=False)
```

time: 64.4 us -> 66.5 us (1.033)
  matrix products: 24.9 us -> 0 us
  Pallas kernels: 0 us -> 22.3 us
  local copies, waits for them, and re-layouts: 8.76 us -> 21.8 us
  other arithmetic: 9.53 us -> 1.73 us
  starting transfers between devices: 14.9 us -> 11 us
  waiting for transfers between devices: 4.86 us -> 8.29 us
    dot_general x6 -> x0, matrix products: 24.9 us -> none  [the longest x1 8.04 us: local(): jnp.einsum('tmlc,tlc->tml', atm_anom, atm_vec, preferred_element_type=jnp...]
    pallas_call x0 -> x3, Pallas kernels: none -> 22.3 us  [the longest x1 14.3 us: local(): pl.pallas_call(functools.partial(first_kernel, per_peer), out_shape=[pltp...]
    unnamed x21 -> x24, local copies, waits for them, and re-layouts: 1.93 us -> 21.8 us
    ppermute x2, waiting for transfers between devices: 0.01 us -> 8.29 us  [the longest x1 8.29 us: local(): low = lax.ppermute(own_high, 'tile', forward)]
    unnamed x7 -> x0, other arithmetic: 7.52 us -> none
    all_to_all x2 -> x1, waiting for transfers between devices: 4.85 us -> 0.01 us  [local(): lax.all_to_all(outgoing, axes, split_axis=0, concat_axis=0, tiled=True)]
    all_to_all x2 -> x1, starting transfers between devices: 10.3 us -> 7.3 us  [local(): lax.all_to_all(outgoing, axes, split_axis=0, concat_axis=0, tiled=True)]
    gather x2 -> x0, local copies, waits for them, and re-layouts: 2.68 us -> none  [the longest x1 1.34 us: local(): jnp.take(atm_proj.reshape(members, flat_width), slot_source, axis=1)]
  transfers between devices with their start and end apart: 4 -> 3, of which waited for: 1 -> 1; matrix products, arithmetic and copies ran while one was open for 39% -> 0% of each run, Pallas kernels for 0% -> 8%
where the time goes in v1:
time: 66.5 us; the launch traced here: 66 us
  Pallas kernels  22.3 us (34%)
  local copies, waits for them, and re-layouts  21.8 us (33%)
  starting transfers between devices  11 us (17%)
  waiting for transfers between devices  8.29 us (12%)
  other arithmetic  1.73 us (3%)
  between operations  0.89 us (1%)
    unnamed x24, local copies, waits for them, and re-layouts  21.8 us
    pallas_call x1, Pallas kernels, local(): pl.pallas_call(functools.partial(first_kernel, per_peer), out_shape=[pltp...  14.3 us
    ppermute x1, waiting for transfers between devices, local(): low = lax.ppermute(own_high, 'tile', forward)  8.29 us
    all_to_all x1, starting transfers between devices, local(): lax.all_to_all(outgoing, axes, split_axis=0, concat_axis=0, tiled=True)  7.3 us
    pallas_call x1, Pallas kernels, local(): pl.pallas_call(second_kernel, out_shape=outs, in_specs=[SMEM_SPEC] * 3 +...  5.34 us
    ppermute x1, starting transfers between devices, local(): high = lax.ppermute(own_low, 'tile', backward)  3.37 us
    pallas_call x1, Pallas kernels, local(): pl.pallas_call(functools.partial(cross_kernel, per_peer), out_shape=outs,...  2.66 us
    concatenate x1, other arithmetic, local(): jnp.concatenate([atm_send.reshape(devices, peer_rows, members), ocn_send....  1.73 us
  transfers between devices with their start and end apart: 3, of which 1 were waited for; matrix products, arithmetic and copies ran while one was open for 0% of the time, Pallas kernels for 8%

profile of v1, /device:TPU:0, one launch (start us, length us, event | category | flops | bytes accessed | tf_op | source)
XLA Modules:
  0.0 66.0 jit_solution(9274400075482560529)
XLA Ops:
  0.6 0.0 copy-start.9
  0.6 0.0 copy-start.11
  0.7 0.0 copy-start.10
  0.7 14.3 %first_pass.1 = (bf16[4,127,80,128]{3,2,1,0:T(8,128)(2,1)S(1)}, bf16[4,75,80,128]{3,2,1,0:T(8,128)(2,1)S(1)}, f32[2,2,80,128]{3,2,1,0:T(8,128)}, f32[2,2,80,128]...) custom-call(s32[4]{0:T(128)} %sea_ref.5, s32[4,128]{1,0:T(4,128)} %pairing_ref.3, ...), custom_call_target="tpu_custom_call" | custom-call | tf_op jit(solution)/shard_map/first_pass/pallas_call | solution.py:299
  15.0 0.0 copy-start.2
  15.0 4.0 %copy-done.2 = bf16[4,127,80,128]{3,2,1,0:T(8,128)(2,1)} copy-done((bf16[4,127,80,128]{3,2,1,0:T(8,128)(2,1)}, bf16[4,127,80,128]{3,2,1,0:T(8,128)(2,1)S(1)}, u32[]{:S(2)}) %copy-start.2) | copy-done | bytes 10403864
  19.0 2.5 %copy-done.4 = bf16[4,75,80,128]{3,2,1,0:T(8,128)(2,1)} copy-done((bf16[4,75,80,128]{3,2,1,0:T(8,128)(2,1)}, bf16[4,75,80,128]{3,2,1,0:T(8,128)(2,1)S(1)}, u32[]{:S(2)}) %copy-start.4) | copy-done | bytes 6144024
  21.5 1.7 %pad_maximum_fusion = bf16[32,32,80]{2,1,0:T(8,128)(2,1)} fusion(bf16[32,16,80]{2,1,0:T(8,128)(2,1)} %bitcast.19, bf16[32,16,80]{2,1,0:T(8,128)(2,1)} %bitcast.18), kind=kLoop, calls=%fused_computation | loop fusion | flops 327680 | bytes 327680 | tf_op jit(solution)/shard_map/concatenate | solution.py:326
  23.3 7.3 %all-to-all-start = ((bf16[32,32,80]{2,1,0:T(8,128)(2,1)}), bf16[32,32,80]{2,1,0:T(8,128)(2,1)S(1)}, u32[]{:S(2)}, u32[]{:S(2)}) async-start(bf16[32,32,80]{2,1,0:T(8,128)(2,1)} %pad_maximum_fusion), calls=%async_computation | async-start | bytes 524288 | tf_op jit(solution)/shard_map/all_to_all | solution.py:333
  30.6 0.3 collective-permute-start
  30.9 3.4 %collective-permute-start.1 = (f32[2,2,80,128]{3,2,1,0:T(8,128)}, f32[2,2,80,128]{3,2,1,0:T(8,128)S(1)}, u32[]{:S(2)}, u32[]{:S(2)}) collective-permute-start(f32[2,2,80,128]{3,2,1,0:T(8,128)} %get-tuple-element.17.own_low_ref), channel_id=1, source_target_pairs={{1,0},{2,1},{3,2},{4,3},{5,4},{6,5},{7,6},{0,7},{9,8},{10,9},{11,1... | collective-permute-start | bytes 491528 | tf_op jit(solution)/shard_map/ppermute | solution.py:324
  34.2 8.3 %collective-permute-done.low_ref = f32[2,2,80,128]{3,2,1,0:T(8,128)S(1)} collective-permute-done((f32[2,2,80,128]{3,2,1,0:T(8,128)}, f32[2,2,80,128]{3,2,1,0:T(8,128)S(1)}, u32[]{:S(2)}, u32[]{:S(2)}) %collective-permute-start) | collective-permute-done | bytes 163872 | tf_op jit(solution)/shard_map/ppermute | solution.py:323
  42.5 0.0 collective-permute-done.1.high_ref
  42.5 0.0 copy-done.9
  42.5 3.9 %copy-done.3 = bf16[4,127,80,128]{3,2,1,0:T(8,128)(2,1)S(1)} copy-done((bf16[4,127,80,128]{3,2,1,0:T(8,128)(2,1)S(1)}, bf16[4,127,80,128]{3,2,1,0:T(8,128)(2,1)}, u32[]{:S(2)}) %copy-start.3) | copy-done | bytes 10403864
  46.5 2.7 %copy-done.5 = bf16[4,75,80,128]{3,2,1,0:T(8,128)(2,1)S(1)} copy-done((bf16[4,75,80,128]{3,2,1,0:T(8,128)(2,1)S(1)}, bf16[4,75,80,128]{3,2,1,0:T(8,128)(2,1)}, u32[]{:S(2)}) %copy-start.5) | copy-done | bytes 6144024
  49.2 0.9 %copy-done.6 = f32[2,2,80,128]{3,2,1,0:T(8,128)S(1)} copy-done((f32[2,2,80,128]{3,2,1,0:T(8,128)S(1)}, f32[2,2,80,128]{3,2,1,0:T(8,128)}, u32[]{:S(2)}) %copy-start.6) | copy-done | bytes 163864
  50.2 0.9 %copy-done.7 = f32[2,2,80,128]{3,2,1,0:T(8,128)S(1)} copy-done((f32[2,2,80,128]{3,2,1,0:T(8,128)S(1)}, f32[2,2,80,128]{3,2,1,0:T(8,128)}, u32[]{:S(2)}) %copy-start.7) | copy-done | bytes 163864
  51.1 5.3 %second_pass.1 = (f32[127,4,128]{2,1,0:T(4,128)}, f32[75,4,128]{2,1,0:T(4,128)}) custom-call(s32[4]{0:T(128)S(1)} %copy-done.9, s32[4,5]{1,0:T(4,128)S(1)} %copy-done.10, s32[4,5]{1,0:T(4,128)S(1)} %copy-done.11, bf16[4,127,80,128]{3,2,1,0:T(8,128)(2,1)S(1)} %copy-done.3, bf16[4,75,80,128]{3,2,1,0:T(8,128)(2,1)S(1)} %copy-done.5, ...), custom_call_target="tpu_custom_call" | custom-call | flops 264765440 | bytes 16547840 | tf_op jit(solution)/shard_map/second_pass/pallas_call | solution.py:342
  56.4 0.0 all-to-all-done
  56.5 0.0 copy-start
  56.5 4.0 %copy-done = bf16[4,80,127,128]{3,1,2,0:T(8,128)(2,1)S(1)} copy-done((bf16[4,80,127,128]{3,1,2,0:T(8,128)(2,1)S(1)}, bf16[4,80,127,128]{3,1,2,0:T(8,128)(2,1)}, u32[]{:S(2)}) %copy-start) | copy-done | bytes 10403864
  60.4 2.7 %copy-done.1 = bf16[4,80,75,128]{3,1,2,0:T(8,128)(2,1)S(1)} copy-done((bf16[4,80,75,128]{3,1,2,0:T(8,128)(2,1)S(1)}, bf16[4,80,75,128]{3,1,2,0:T(8,128)(2,1)}, u32[]{:S(2)}) %copy-start.1) | copy-done | bytes 6144024
  63.2 2.7 %surface_cross.1 = (f32[127,4,128]{2,1,0:T(4,128)}, f32[75,4,128]{2,1,0:T(4,128)}) custom-call(s32[4]{0:T(128)S(1)} %copy-done.9, s32[4,128]{1,0:T(4,128)S(1)} %copy-done.8, bf16[512,80]{1,0:T(8,128)(2,1)S(1)} %bitcast.15, bf16[512,80]{1,0:T(8,128)(2,1)S(1)} %bitcast.14, ...), custom_call_target="tpu_custom_call", output_to_operand_aliasing={{0}: (6, {}), {1}: (7, {})} | custom-call | tf_op jit(solution)/shard_map/surface_cross/pallas_call | solution.py:355
  (11 shorter events, 0.0 us)
Async XLA Ops:
  0.6 41.9 %copy-start.9 = (s32[4]{0:T(128)S(1)}, s32[4]{0:T(128)}, u32[]{:S(2)}) copy-start(s32[4]{0:T(128)} %sea_ref.5) | copy-start | bytes 52
  0.6 41.9 %copy-start.11 = (s32[4,5]{1,0:T(4,128)S(1)}, s32[4,5]{1,0:T(4,128)}, u32[]{:S(2)}) copy-start(s32[4,5]{1,0:T(4,128)} %ocn_class_ref.1) | copy-start | bytes 244
  0.7 41.9 %copy-start.10 = (s32[4,5]{1,0:T(4,128)S(1)}, s32[4,5]{1,0:T(4,128)}, u32[]{:S(2)}) copy-start(s32[4,5]{1,0:T(4,128)} %atm_class_ref.1) | copy-start | bytes 244
  15.0 4.0 %copy-start.2 = (bf16[4,127,80,128]{3,2,1,0:T(8,128)(2,1)}, bf16[4,127,80,128]{3,2,1,0:T(8,128)(2,1)S(1)}, u32[]{:S(2)}) copy-start(bf16[4,127,80,128]{3,2,1,0:T(8,128)(2,1)S(1)} %get-tuple-element.14.atm_ref) | copy-start | bytes 31211524
  19.0 2.5 %copy-start.4 = (bf16[4,75,80,128]{3,2,1,0:T(8,128)(2,1)}, bf16[4,75,80,128]{3,2,1,0:T(8,128)(2,1)S(1)}, u32[]{:S(2)}) copy-start(bf16[4,75,80,128]{3,2,1,0:T(8,128)(2,1)S(1)} %get-tuple-element.15.ocn_ref) | copy-start | bytes 18432004
  21.5 34.9 %copy-start.8 = (s32[4,128]{1,0:T(4,128)S(1)}, s32[4,128]{1,0:T(4,128)}, u32[]{:S(2)}) copy-start(s32[4,128]{1,0:T(4,128)} %pairing_ref.3) | copy-start | bytes 6148
  23.3 33.2 %all-to-all-start = ((bf16[32,32,80]{2,1,0:T(8,128)(2,1)}), bf16[32,32,80]{2,1,0:T(8,128)(2,1)S(1)}, u32[]{:S(2)}, u32[]{:S(2)}) async-start(bf16[32,32,80]{2,1,0:T(8,128)(2,1)} %pad_maximum_fusion), calls=%async_computation | async-start | bytes 524288 | tf_op jit(solution)/shard_map/all_to_all | solution.py:333
  30.6 12.0 %collective-permute-start = (f32[2,2,80,128]{3,2,1,0:T(8,128)}, f32[2,2,80,128]{3,2,1,0:T(8,128)S(1)}, u32[]{:S(2)}, u32[]{:S(2)}) collective-permute-start(f32[2,2,80,128]{3,2,1,0:T(8,128)} %get-tuple-element.16.own_high_ref), channel_id=1, source_target_pairs={{0,1},{1,2},{2,3},{3,4},{4,5},{5,6},{6,7},{7,0},{8,9},{9,10},{10,1... | collective-permute-start | bytes 491528 | tf_op jit(solution)/shard_map/ppermute | solution.py:323
  30.9 11.7 %collective-permute-start.1 = (f32[2,2,80,128]{3,2,1,0:T(8,128)}, f32[2,2,80,128]{3,2,1,0:T(8,128)S(1)}, u32[]{:S(2)}, u32[]{:S(2)}) collective-permute-start(f32[2,2,80,128]{3,2,1,0:T(8,128)} %get-tuple-element.17.own_low_ref), channel_id=1, source_target_pairs={{1,0},{2,1},{3,2},{4,3},{5,4},{6,5},{7,6},{0,7},{9,8},{10,9},{11,1... | collective-permute-start | bytes 491528 | tf_op jit(solution)/shard_map/ppermute | solution.py:324
  42.5 4.0 %copy-start.3 = (bf16[4,127,80,128]{3,2,1,0:T(8,128)(2,1)S(1)}, bf16[4,127,80,128]{3,2,1,0:T(8,128)(2,1)}, u32[]{:S(2)}) copy-start(bf16[4,127,80,128]{3,2,1,0:T(8,128)(2,1)} %copy-done.2) | copy-start | bytes 31211524
  46.5 2.7 %copy-start.5 = (bf16[4,75,80,128]{3,2,1,0:T(8,128)(2,1)S(1)}, bf16[4,75,80,128]{3,2,1,0:T(8,128)(2,1)}, u32[]{:S(2)}) copy-start(bf16[4,75,80,128]{3,2,1,0:T(8,128)(2,1)} %copy-done.4) | copy-start | bytes 18432004
  49.2 0.9 %copy-start.6 = (f32[2,2,80,128]{3,2,1,0:T(8,128)S(1)}, f32[2,2,80,128]{3,2,1,0:T(8,128)}, u32[]{:S(2)}) copy-start(f32[2,2,80,128]{3,2,1,0:T(8,128)} %get-tuple-element.16.own_high_ref) | copy-start | bytes 491524
  50.2 0.9 %copy-start.7 = (f32[2,2,80,128]{3,2,1,0:T(8,128)S(1)}, f32[2,2,80,128]{3,2,1,0:T(8,128)}, u32[]{:S(2)}) copy-start(f32[2,2,80,128]{3,2,1,0:T(8,128)} %get-tuple-element.17.own_low_ref) | copy-start | bytes 491524
  56.5 4.0 %copy-start = (bf16[4,80,127,128]{3,1,2,0:T(8,128)(2,1)S(1)}, bf16[4,80,127,128]{3,1,2,0:T(8,128)(2,1)}, u32[]{:S(2)}) copy-start(bf16[4,80,127,128]{3,1,2,0:T(8,128)(2,1)} %param.8) | copy-start | bytes 31211524
  60.4 2.7 %copy-start.1 = (bf16[4,80,75,128]{3,1,2,0:T(8,128)(2,1)S(1)}, bf16[4,80,75,128]{3,1,2,0:T(8,128)(2,1)}, u32[]{:S(2)}) copy-start(bf16[4,80,75,128]{3,1,2,0:T(8,128)(2,1)} %param.9) | copy-start | bytes 18432004

commit v2 on v1

v2 whole, which is shorter than its diff:
```python
import functools
import math

import jax
import jax.numpy as jnp
from jax import lax
from jax.experimental import pallas as pl
from jax.experimental.pallas import tpu as pltpu
from jax.sharding import PartitionSpec as P

KA = 16
KO = 16
HALO = 2
GROUP = 8

COUPLING = 8.0
ATM_SPREAD = 12.0
OCN_SPREAD = 8.0
CLASS_TABLE = (1.0, 0.7, 0.45, 0.25, 0.0)

BF16 = jnp.bfloat16
F32 = jnp.float32
MIB = 1 << 20
NT = (((1,), (1,)), ((), ()))
TN = (((0,), (0,)), ((), ()))
VMEM_SPEC = pl.BlockSpec(memory_space=pltpu.VMEM)
SMEM_SPEC = pl.BlockSpec(memory_space=pltpu.SMEM)
ANY_SPEC = pl.BlockSpec(memory_space=pl.ANY)

RISE = [math.exp(-2.0 * (KA - 1 - s) / KA) for s in range(KA)]
FALL = [math.exp(-2.0 * o / KO) for o in range(KO)]


def slot_rows(index, columns, tiles, per_peer):
    tile, column = index // columns, index % columns
    return (tile // tiles) * (tiles * per_peer) + (tile % tiles) * per_peer + column % per_peer


def one_hot(rows, width):
    position = lax.broadcasted_iota(jnp.int32, (width, rows.shape[1]), 0)
    return jnp.where(position == rows, 1.0, 0.0).astype(BF16)


def atm_slots(pairing_ref, columns, tiles, per_peer):
    index = jnp.concatenate([pairing_ref[t : t + 1, :] for t in range(tiles)], axis=1)
    return one_hot(slot_rows(index, columns, tiles, per_peer), tiles * columns)


def ocn_slots(columns, tiles, per_peer):
    place = lax.broadcasted_iota(jnp.int32, (1, tiles * columns), 1)
    tile, column = place // columns, place % columns
    rows = (column // per_peer) * (tiles * per_peer) + tile * per_peer + column % per_peer
    return one_hot(rows, tiles * columns)


def in_vmem(array):
    return pltpu.with_memory_space_constraint(array, pltpu.VMEM)


def tile_copies(source, target, sems):
    return [
        pltpu.make_async_copy(source.at[t], target.at[t], sems.at[t]) for t in range(source.shape[0])
    ]


def spread_vectors(source, vec_ref, which, tiles):
    levels, _, columns = source.shape
    for t in range(tiles):
        place = which * tiles + t
        vec_ref[place, :levels] = source[:, t, :].astype(F32)
        if levels < columns:
            vec_ref[place, levels:] = jnp.zeros((columns - levels, columns), F32)


def project_kernel(
    per_peer,
    sea_hbm,
    pairing_hbm,
    atm_vec_hbm,
    ocn_vec_hbm,
    atm_hbm,
    ocn_hbm,
    send_ref,
    atm_top,
    ocn_top,
    sems,
    sea_ref,
    pairing_ref,
    atm_vec_ref,
    ocn_vec_ref,
    small_sems,
):
    tiles, atm_levels, members, columns = atm_hbm.shape
    start = atm_levels - KA
    peers, count = send_ref.shape[0], send_ref.shape[1] // 2
    small = [
        pltpu.make_async_copy(pairing_hbm, pairing_ref, small_sems.at[0]),
        pltpu.make_async_copy(atm_vec_hbm.at[pl.ds(start, KA)], atm_vec_ref, small_sems.at[1]),
        pltpu.make_async_copy(ocn_vec_hbm.at[pl.ds(0, KO)], ocn_vec_ref, small_sems.at[2]),
        pltpu.make_async_copy(sea_hbm, sea_ref, small_sems.at[3]),
    ]
    for load in small:
        load.start()
    loads = [
        [
            pltpu.make_async_copy(atm_hbm.at[t, pl.ds(start, KA)], atm_top.at[t], sems.at[0, t]),
            pltpu.make_async_copy(ocn_hbm.at[t, pl.ds(0, KO)], ocn_top.at[t], sems.at[1, t]),
        ]
        for t in range(tiles)
    ]
    for pair in loads:
        for load in pair:
            load.start()
    for load in small:
        load.wait()
    slots = [
        atm_slots(pairing_ref, columns, tiles, per_peer),
        ocn_slots(columns, tiles, per_peer),
    ]
    atm_rows = atm_vec_ref[...].astype(F32)
    ocn_rows = ocn_vec_ref[...].astype(F32)

    def projection(top, t, rows, weights):
        total = jnp.zeros((members, columns), F32)
        for s, weight in enumerate(weights):
            total = total + top[t, s].astype(F32) * (rows[s, t : t + 1, :] * weight)
        return total

    atm_proj, ocn_proj = [], []
    for t in range(tiles):
        for load in loads[t]:
            load.wait()
        atm_proj.append(projection(atm_top, t, atm_rows, RISE).astype(BF16))
        sea = sea_ref[t].astype(F32)
        ocn_proj.append((projection(ocn_top, t, ocn_rows, FALL) * sea).astype(BF16))
    for place, proj in enumerate([atm_proj, ocn_proj]):
        rows = lax.dot_general(
            slots[place], jnp.concatenate(proj, axis=1), NT, preferred_element_type=F32
        ).astype(BF16)
        send_ref[:, place * count : (place + 1) * count, :] = rows.reshape(peers, count, members)


def first_kernel(
    sea_hbm,
    atm_vec_hbm,
    ocn_vec_hbm,
    atm_hbm,
    ocn_hbm,
    inner_ref,
    outer_ref,
    atm_ref,
    ocn_ref,
    sea_ref,
    atm_vec_ref,
    ocn_vec_ref,
    vec_ref,
    weight_ref,
    small_sems,
    atm_sems,
    ocn_sems,
):
    tiles, atm_levels, members, columns = atm_hbm.shape
    ocn_levels = ocn_hbm.shape[1]
    small = [
        pltpu.make_async_copy(atm_vec_hbm, atm_vec_ref, small_sems.at[0]),
        pltpu.make_async_copy(ocn_vec_hbm, ocn_vec_ref, small_sems.at[1]),
        pltpu.make_async_copy(sea_hbm, sea_ref, small_sems.at[2]),
    ]
    for load in small:
        load.start()
    atm_copies = tile_copies(atm_hbm, atm_ref, atm_sems)
    ocn_copies = tile_copies(ocn_hbm, ocn_ref, ocn_sems)
    for copy in atm_copies + ocn_copies:
        copy.start()
    even = lax.rem(lax.axis_index("tile"), 2) == 0
    lane = lax.broadcasted_iota(jnp.int32, (members, columns), 1)

    zeros = jnp.zeros((columns, columns), BF16)
    for load in small:
        load.wait()
    spread_vectors(atm_vec_ref, vec_ref, 0, tiles)
    spread_vectors(ocn_vec_ref, vec_ref, 1, tiles)
    for place in range(2 * tiles):
        vec_t = vec_ref[place].T.astype(BF16)
        weight_ref[place, :columns, :columns] = vec_t
        weight_ref[place, :columns, columns:] = zeros
        weight_ref[place, columns:, :columns] = zeros
        weight_ref[place, columns:, columns:] = vec_t

    def coefficients(ref, t, place, levels):
        half = (levels + 1) // 2
        second = levels - half
        total = jnp.zeros((members, columns), F32)
        for first in range(0, half, GROUP):
            count = min(GROUP, half - first)
            left = ref[t, first : first + count].reshape(count * members, columns)
            right = ref[t, second + first : second + first + count].reshape(count * members, columns)
            product = jnp.dot(
                jnp.concatenate([left, right], axis=1),
                weight_ref[place],
                preferred_element_type=F32,
            )
            for j in range(count):
                part = product[j * members : (j + 1) * members]
                total = jnp.where(lane == first + j, part[:, :columns], total)
                total = jnp.where(lane == second + first + j, part[:, columns:], total)
        return total

    def store(t, which, value):
        lower = t < tiles // 2
        slot = t if lower else t - tiles // 2

        @pl.when(jnp.logical_not(even) if lower else even)
        def _():
            inner_ref[slot, which] = value

        @pl.when(even if lower else jnp.logical_not(even))
        def _():
            outer_ref[slot, which] = value

    for t in range(tiles):
        atm_copies[t].wait()
        store(t, 0, coefficients(atm_ref, t, t, atm_levels))
    for t in range(tiles):
        ocn_copies[t].wait()
        sea = sea_ref[t].astype(F32)
        store(t, 1, coefficients(ocn_ref, t, tiles + t, ocn_levels) * sea)


def second_kernel(
    sea_ref,
    atm_class_ref,
    ocn_class_ref,
    inner_ref,
    outer_ref,
    inner_recv_ref,
    outer_recv_ref,
    atm_cross_ref,
    ocn_cross_ref,
    atm_hbm,
    ocn_hbm,
    atm_out_hbm,
    ocn_out_hbm,
    atm_ref,
    ocn_ref,
    atm_out_ref,
    ocn_out_ref,
    padded_ref,
    vert_ref,
    out_sems,
    atm_sems,
    ocn_sems,
):
    tiles, atm_levels, members, columns = atm_hbm.shape
    ocn_levels = ocn_hbm.shape[1]
    atm_copies = tile_copies(atm_hbm, atm_ref, atm_sems)
    ocn_copies = tile_copies(ocn_hbm, ocn_ref, ocn_sems)
    for copy in atm_copies + ocn_copies:
        copy.start()
    even = lax.rem(lax.axis_index("tile"), 2) == 0
    quarter = tiles // 2

    @pl.when(even)
    def _():
        for place, ref in enumerate([outer_recv_ref, outer_ref, inner_ref, inner_recv_ref]):
            padded_ref[place * quarter : (place + 1) * quarter] = ref[...]

    @pl.when(jnp.logical_not(even))
    def _():
        for place, ref in enumerate([inner_recv_ref, inner_ref, outer_ref, outer_recv_ref]):
            padded_ref[place * quarter : (place + 1) * quarter] = ref[...]

    group = 16
    sub = lax.broadcasted_iota(jnp.int32, (group, columns), 0)
    row = lax.broadcasted_iota(jnp.int32, (columns, columns), 0)
    col = lax.broadcasted_iota(jnp.int32, (columns, columns), 1)

    def class_weight(number):
        weight = jnp.float32(0.0)
        for value, factor in enumerate(CLASS_TABLE):
            weight = jnp.where(number == value, jnp.float32(factor), weight)
        return weight

    def taper(spread):
        scaled = (row - col).astype(F32) * (1.0 / spread)
        return jnp.exp(-0.5 * scaled * scaled)

    stores = [
        pltpu.make_async_copy(atm_out_ref, atm_out_hbm, out_sems.at[0]),
        pltpu.make_async_copy(ocn_out_ref, ocn_out_hbm, out_sems.at[1]),
    ]
    parts = [
        (atm_ref, atm_copies, atm_out_ref, atm_class_ref, atm_levels, ATM_SPREAD),
        (ocn_ref, ocn_copies, ocn_out_ref, ocn_class_ref, ocn_levels, OCN_SPREAD),
    ]
    for which, (_, _, _, class_ref, _, width) in enumerate(parts):
        tapering = taper(width)
        for t in range(tiles):
            spread = jnp.zeros((members, columns), F32)
            for offset in range(2 * HALO + 1):
                spread = spread + class_weight(class_ref[t, offset]) * padded_ref[t + offset, which]
            vert_ref[which, t] = lax.dot_general(
                tapering, spread, NT, precision=lax.Precision.HIGHEST, preferred_element_type=F32
            ).astype(BF16)

    for which, (ref, copies, out_ref, _, levels, _) in enumerate(parts):
        for t in range(tiles):
            copies[t].wait()
            for start in range(0, levels, group):
                count = min(group, levels - start)
                right = jnp.concatenate([ref[t, start + j] for j in range(count)], axis=1)
                product = jnp.dot(
                    vert_ref[which, t, start : start + group, :], right, preferred_element_type=F32
                )
                total = product[:, :columns]
                for j in range(1, count):
                    total = jnp.where(sub == j, product[:, j * columns : (j + 1) * columns], total)
                if which == 1:
                    total = total * sea_ref[t].astype(F32)
                out_ref[start : start + count, t, :] = total[:count]
        if which == 0:
            surface = levels - KA
            out_ref[surface:] = out_ref[surface:] + atm_cross_ref[...]
        else:
            out_ref[:KO] = out_ref[:KO] + ocn_cross_ref[...]
        stores[which].start()
    for store in stores:
        store.wait()


def cross_kernel(
    per_peer,
    sea_ref,
    pairing_ref,
    recv_ref,
    atm_hbm,
    ocn_hbm,
    atm_cross_ref,
    ocn_cross_ref,
    atm_top,
    ocn_top,
    sems,
):
    tiles, atm_levels, members, columns = atm_hbm.shape
    start = atm_levels - KA
    loads = [
        [
            pltpu.make_async_copy(atm_hbm.at[t, pl.ds(start, KA)], atm_top.at[t], sems.at[0, t]),
            pltpu.make_async_copy(ocn_hbm.at[t, pl.ds(0, KO)], ocn_top.at[t], sems.at[1, t]),
        ]
        for t in range(tiles)
    ]
    for pair in loads:
        for load in pair:
            load.start()
    peers, count = recv_ref.shape[0], recv_ref.shape[1] // 2

    def pair_columns(first, slots):
        rows = recv_ref[:, first : first + count, :].reshape(peers * count, members)
        return lax.dot_general(rows, slots, TN, preferred_element_type=F32)

    atm_pair = pair_columns(count, atm_slots(pairing_ref, columns, tiles, per_peer))
    ocn_pair = pair_columns(0, ocn_slots(columns, tiles, per_peer))

    def rows_of(top, t, paired, weights):
        part = paired[:, t * columns : (t + 1) * columns]
        sums = [
            jnp.sum(top[t, s].astype(F32) * part, axis=0, keepdims=True) * (COUPLING * weight)
            for s, weight in enumerate(weights)
        ]
        return jnp.concatenate(sums, axis=0)

    for t in range(tiles):
        for load in loads[t]:
            load.wait()
        atm_cross_ref[:, t, :] = rows_of(atm_top, t, atm_pair, RISE)
        ocn_cross_ref[:, t, :] = rows_of(ocn_top, t, ocn_pair, FALL) * sea_ref[t].astype(F32)


def local(atm_anom, ocn_anom, atm_vec, ocn_vec, atm_to_ocean, sea_tiles, atm_class, ocn_class):
    tiles, members, atm_levels, columns = atm_anom.shape
    ocn_levels = ocn_anom.shape[2]
    axes = ("dom", "tile")
    devices = lax.axis_size("dom") * lax.axis_size("tile")
    per_peer = columns // devices
    peer_rows = tiles * per_peer

    by_level = (0, 2, 1, 3)
    atm = jnp.transpose(atm_anom, by_level)
    ocn = jnp.transpose(ocn_anom, by_level)
    atm_rows = jnp.transpose(atm_vec, (1, 0, 2))
    ocn_rows = jnp.transpose(ocn_vec, (1, 0, 2))
    params = pltpu.CompilerParams(vmem_limit_bytes=58 * MIB)

    elements = tiles * members * columns * (atm_levels + ocn_levels)
    top_elements = tiles * members * columns * (KA + KO)
    tops = [
        pltpu.VMEM((tiles, KA, members, columns), BF16),
        pltpu.VMEM((tiles, KO, members, columns), BF16),
        pltpu.SemaphoreType.DMA((2, tiles)),
    ]
    wholes = [pltpu.VMEM(atm.shape, BF16), pltpu.VMEM(ocn.shape, BF16)]
    whole_sems = [pltpu.SemaphoreType.DMA((tiles,)), pltpu.SemaphoreType.DMA((tiles,))]

    def cost(flops, count):
        return pl.CostEstimate(flops=flops, bytes_accessed=2 * count, transcendentals=0)

    outgoing = pl.pallas_call(
        functools.partial(project_kernel, per_peer),
        out_shape=pltpu.VMEM((devices, 2 * peer_rows, members), BF16),
        in_specs=[ANY_SPEC] * 6,
        out_specs=VMEM_SPEC,
        scratch_shapes=tops
        + [
            pltpu.SMEM(sea_tiles.shape, jnp.int32),
            pltpu.VMEM(atm_to_ocean.shape, jnp.int32),
            pltpu.VMEM((KA, tiles, columns), BF16),
            pltpu.VMEM((KO, tiles, columns), BF16),
            pltpu.SemaphoreType.DMA((4,)),
        ],
        compiler_params=params,
        cost_estimate=cost(4 * top_elements, top_elements),
        name="project",
    )(sea_tiles, atm_to_ocean, atm_rows, ocn_rows, atm, ocn)
    incoming = lax.all_to_all(outgoing, axes, split_axis=0, concat_axis=0, tiled=True)

    edge = pltpu.VMEM((tiles // 2, 2, members, columns), F32)
    inner, outer = pl.pallas_call(
        first_kernel,
        out_shape=[edge, edge],
        in_specs=[ANY_SPEC] * 5,
        out_specs=[VMEM_SPEC] * 2,
        scratch_shapes=wholes
        + [
            pltpu.SMEM(sea_tiles.shape, jnp.int32),
            pltpu.VMEM(atm_rows.shape, BF16),
            pltpu.VMEM(ocn_rows.shape, BF16),
            pltpu.VMEM((2 * tiles, columns, columns), F32),
            pltpu.VMEM((2 * tiles, 2 * columns, 2 * columns), BF16),
            pltpu.SemaphoreType.DMA((3,)),
        ]
        + whole_sems,
        compiler_params=params,
        cost_estimate=cost(2 * 256 * elements, elements),
        name="first_pass",
    )(sea_tiles, atm_rows, ocn_rows, atm, ocn)

    count = lax.axis_size("tile")
    outer_pairs = [(i, (i + 1) % count if i % 2 else (i - 1) % count) for i in range(count)]
    outer_recv = lax.ppermute(outer, "tile", outer_pairs)
    inner_recv = lax.ppermute(inner, "tile", [(i, i ^ 1) for i in range(count)])

    atm_cross, ocn_cross = pl.pallas_call(
        functools.partial(cross_kernel, per_peer),
        out_shape=[
            pltpu.VMEM((KA, tiles, columns), F32),
            pltpu.VMEM((KO, tiles, columns), F32),
        ],
        in_specs=[SMEM_SPEC, VMEM_SPEC, VMEM_SPEC] + [ANY_SPEC] * 2,
        out_specs=[VMEM_SPEC] * 2,
        scratch_shapes=tops,
        compiler_params=params,
        cost_estimate=cost(40 * top_elements, 4 * top_elements),
        name="surface_cross",
    )(sea_tiles, atm_to_ocean, in_vmem(incoming), atm, ocn)

    atm_out, ocn_out = pl.pallas_call(
        second_kernel,
        out_shape=[
            jax.ShapeDtypeStruct((atm_levels, tiles, columns), F32),
            jax.ShapeDtypeStruct((ocn_levels, tiles, columns), F32),
        ],
        in_specs=[SMEM_SPEC] * 3 + [VMEM_SPEC] * 6 + [ANY_SPEC] * 2,
        out_specs=[ANY_SPEC] * 2,
        scratch_shapes=wholes
        + [
            pltpu.VMEM((atm_levels, tiles, columns), F32),
            pltpu.VMEM((ocn_levels, tiles, columns), F32),
            pltpu.VMEM((2 * tiles, 2, members, columns), F32),
            pltpu.VMEM((2, tiles, columns, members), BF16),
            pltpu.SemaphoreType.DMA((2,)),
        ]
        + whole_sems,
        compiler_params=params,
        cost_estimate=cost(2 * 256 * elements, elements),
        name="second_pass",
    )(
        sea_tiles,
        atm_class,
        ocn_class,
        in_vmem(inner),
        in_vmem(outer),
        in_vmem(inner_recv),
        in_vmem(outer_recv),
        in_vmem(atm_cross),
        in_vmem(ocn_cross),
        atm,
        ocn,
    )
    return jnp.transpose(atm_out, (1, 0, 2)), jnp.transpose(ocn_out, (1, 0, 2))


def solution(mesh):
    in_specs = (
        P(("dom", "tile"), None, None, None),
        P(("dom", "tile"), None, None, None),
        P(("dom", "tile"), None, None),
        P(("dom", "tile"), None, None),
        P(("dom", "tile"), None),
        P(("dom", "tile")),
        P(("dom", "tile"), None),
        P(("dom", "tile"), None),
    )
    out_specs = (P(("dom", "tile"), None, None), P(("dom", "tile"), None, None))
    return jax.shard_map(local, mesh=mesh, in_specs=in_specs, out_specs=out_specs, check_vma=False)
```

time: 66.5 us -> 38.3 us (0.58)
  local copies, waits for them, and re-layouts: 21.8 us -> 0 us
  waiting for transfers between devices: 8.29 us -> 1.43 us
  Pallas kernels: 22.3 us -> 24.8 us
  other arithmetic: 1.73 us -> 0 us
    unnamed x24 -> x0, local copies, waits for them, and re-layouts: 21.8 us -> none
    ppermute x2, waiting for transfers between devices: 8.29 us -> 1.43 us  [the longest x1 1.43 us: local(): outer_recv = lax.ppermute(outer, 'tile', outer_pairs)]
    pallas_call x3 -> x4, Pallas kernels: 22.3 us -> 24.8 us  [the longest x1 10.2 us: local(): pl.pallas_call(first_kernel, out_shape=[edge, edge], in_specs=[ANY_SPEC]...]
    concatenate x1 -> x0, other arithmetic: 1.73 us -> none  [local(): jnp.concatenate([atm_send.reshape(devices, peer_rows, members), ocn_send....]
  transfers between devices with their start and end apart: 3 -> 3, of which waited for: 1 -> 1; matrix products, arithmetic and copies ran while one was open for 0% -> 0% of each run, Pallas kernels for 8% -> 34%
where the time goes in v2:
time: 38.3 us; the launch traced here: 38 us
  Pallas kernels  24.8 us (65%)
  starting transfers between devices  11.1 us (29%)
  waiting for transfers between devices  1.43 us (4%)
  between operations  0.67 us (2%)
    pallas_call x1, Pallas kernels, local(): pl.pallas_call(first_kernel, out_shape=[edge, edge], in_specs=[ANY_SPEC]...  10.2 us
    pallas_call x1, Pallas kernels, local(): pl.pallas_call(second_kernel, out_shape=[jax.ShapeDtypeStruct((atm_levels...  8.63 us
    all_to_all x1, starting transfers between devices, local(): lax.all_to_all(outgoing, axes, split_axis=0, concat_axis=0, tiled=True)  7.3 us
    ppermute x1, starting transfers between devices, local(): outer_recv = lax.ppermute(outer, 'tile', outer_pairs)  3.48 us
    pallas_call x1, Pallas kernels, local(): pl.pallas_call(functools.partial(project_kernel, per_peer), out_shape=plt...  3.36 us
    pallas_call x1, Pallas kernels, local(): pl.pallas_call(functools.partial(cross_kernel, per_peer), out_shape=[pltp...  2.66 us
    ppermute x1, waiting for transfers between devices, local(): outer_recv = lax.ppermute(outer, 'tile', outer_pairs)  1.43 us
  transfers between devices with their start and end apart: 3, of which 1 were waited for; matrix products, arithmetic and copies ran while one was open for 0% of the time, Pallas kernels for 34%

profile of v2, /device:TPU:0, one launch (start us, length us, event | category | flops | bytes accessed | tf_op | source)
XLA Modules:
  0.0 38.0 jit_solution(3981690114442068616)
XLA Ops:
  0.6 3.4 %project.1 = bf16[32,32,80]{2,1,0:T(8,128)(2,1)} custom-call(s32[4]{0:T(128)} %sea_ref.3, s32[4,128]{1,0:T(4,128)} %pairing_ref.1, bf16[127,4,128]{2,1,0:T(4,128)(2,1)} %bitcast.14, bf16[75,4,128]{2,1,0:T(4,128)(2,1)} %bitcast.16, bf16[4,127,80,128]{3,2,1,0:T(8,128)(2,1)} %bitcast.6, bf16[4,75,80,128]{3,2,1,0:T(8,128)(2,1)} %bitcast.10), custom_call_target="tpu_custom_call" | custom-call | flops 5242880 | bytes 2621440 | tf_op jit(solution)/shard_map/project/pallas_call | solution.py:408
  4.0 7.3 %all-to-all-start = ((bf16[32,32,80]{2,1,0:T(8,128)(2,1)}), bf16[32,32,80]{2,1,0:T(8,128)(2,1)S(1)}, u32[]{:S(2)}, u32[]{:S(2)}) async-start(bf16[32,32,80]{2,1,0:T(8,128)(2,1)} %project.1), calls=%async_computation | async-start | bytes 524288 | tf_op jit(solution)/shard_map/all_to_all | solution.py:425
  11.3 10.2 %first_pass.1 = (f32[2,2,80,128]{3,2,1,0:T(8,128)S(1)}, f32[2,2,80,128]{3,2,1,0:T(8,128)S(1)}) custom-call(s32[4]{0:T(128)} %sea_ref.3, bf16[127,4,128]{2,1,0:T(4,128)(2,1)} %bitcast.15, bf16[75,4,128]{2,1,0:T(4,128)(2,1)} %bitcast.17, bf16[4,127,80,128]{3,2,1,0:T(8,128)(2,1)} %bitcast.7, bf16[4,75,80,128]{3,2,1,0:T(8,128)(2,1)} %bitcast.11), custom_call_target="tpu_custom_call" | custom-call | flops 4236247040 | bytes 16547840 | tf_op jit(solution)/shard_map/first_pass/pallas_call | solution.py:428
  21.5 0.3 collective-permute-start
  21.8 3.5 %collective-permute-start.1 = (f32[2,2,80,128]{3,2,1,0:T(8,128)S(1)}, f32[2,2,80,128]{3,2,1,0:T(8,128)S(1)}, u32[]{:S(2)}, u32[]{:S(2)}) collective-permute-start(f32[2,2,80,128]{3,2,1,0:T(8,128)S(1)} %get-tuple-element.9.outer_ref), channel_id=1, source_target_pairs={{0,7},{1,2},{2,1},{3,4},{4,3},{5,6},{6,5},{7,0},{8,15},{9,10},{10,... | collective-permute-start | bytes 491528 | tf_op jit(solution)/shard_map/ppermute | solution.py:450
  25.3 0.0 all-to-all-done.recv_ref
  25.3 2.7 %surface_cross.1 = (f32[16,4,128]{2,1,0:T(4,128)S(1)}, f32[16,4,128]{2,1,0:T(4,128)S(1)}) custom-call(s32[4]{0:T(128)} %sea_ref.3, s32[4,128]{1,0:T(4,128)} %pairing_ref.1, bf16[32,32,80]{2,1,0:T(8,128)(2,1)S(1)} %all-to-all-done.recv_ref, bf16[4,127,80,128]{3,2,1,0:T(8,128)(2,1)} %bitcast.8, bf16[4,75,80,128]{3,2,1,0:T(8,128)(2,1)} %bitcast.12), custom_call_target="tpu_custom_call" | custom-call | flops 52428800 | bytes 10485760 | tf_op jit(solution)/shard_map/surface_cross/pallas_call | solution.py:453
  27.9 0.0 collective-permute-done.inner_recv_ref
  28.0 1.4 %collective-permute-done.1.outer_recv_ref = f32[2,2,80,128]{3,2,1,0:T(8,128)S(1)} collective-permute-done((f32[2,2,80,128]{3,2,1,0:T(8,128)S(1)}, f32[2,2,80,128]{3,2,1,0:T(8,128)S(1)}, u32[]{:S(2)}, u32[]{:S(2)}) %collective-permute-start.1) | collective-permute-done | bytes 163872 | tf_op jit(solution)/shard_map/ppermute | solution.py:450
  29.4 8.6 %second_pass.1 = (f32[127,4,128]{2,1,0:T(4,128)}, f32[75,4,128]{2,1,0:T(4,128)}) custom-call(s32[4]{0:T(128)} %sea_ref.3, s32[4,5]{1,0:T(4,128)} %atm_class_ref.1, s32[4,5]{1,0:T(4,128)} %ocn_class_ref.1, f32[2,2,80,128]{3,2,1,0:T(8,128)S(1)} %get-tuple-element.8.inner_ref, f32[2,2,80,128]{3,2,1,0:T(8,128)S(1)} %get-tuple-element.9.outer_ref, ...), custom_call_target="tpu_custom_call" | custom-call | flops 4236247040 | bytes 16547840 | tf_op jit(solution)/shard_map/second_pass/pallas_call | solution.py:467
Async XLA Ops:
  4.0 21.3 %all-to-all-start = ((bf16[32,32,80]{2,1,0:T(8,128)(2,1)}), bf16[32,32,80]{2,1,0:T(8,128)(2,1)S(1)}, u32[]{:S(2)}, u32[]{:S(2)}) async-start(bf16[32,32,80]{2,1,0:T(8,128)(2,1)} %project.1), calls=%async_computation | async-start | bytes 524288 | tf_op jit(solution)/shard_map/all_to_all | solution.py:425
  21.5 6.5 %collective-permute-start = (f32[2,2,80,128]{3,2,1,0:T(8,128)S(1)}, f32[2,2,80,128]{3,2,1,0:T(8,128)S(1)}, u32[]{:S(2)}, u32[]{:S(2)}) collective-permute-start(f32[2,2,80,128]{3,2,1,0:T(8,128)S(1)} %get-tuple-element.8.inner_ref), channel_id=1, source_target_pairs={{0,1},{1,0},{2,3},{3,2},{4,5},{5,4},{6,7},{7,6},{8,9},{9,8},{10,11... | collective-permute-start | bytes 491528 | tf_op jit(solution)/shard_map/ppermute | solution.py:451
  21.8 7.6 %collective-permute-start.1 = (f32[2,2,80,128]{3,2,1,0:T(8,128)S(1)}, f32[2,2,80,128]{3,2,1,0:T(8,128)S(1)}, u32[]{:S(2)}, u32[]{:S(2)}) collective-permute-start(f32[2,2,80,128]{3,2,1,0:T(8,128)S(1)} %get-tuple-element.9.outer_ref), channel_id=1, source_target_pairs={{0,7},{1,2},{2,1},{3,4},{4,3},{5,6},{6,5},{7,0},{8,15},{9,10},{10,... | collective-permute-start | bytes 491528 | tf_op jit(solution)/shard_map/ppermute | solution.py:450

commit v3 on v2

--- a/solution.py
+++ b/solution.py
@@ -12,6 +12,8 @@
 KO = 16
 HALO = 2
 GROUP = 8
+ATM_REGIONS = [[0], [1], [2], [3]]
+REGIONS = [[(0, 0)], [(0, 1), (0, 2)], [(0, 3), (1, 0)], [(1, 1), (1, 2), (1, 3)]]
 
 COUPLING = 8.0
 ATM_SPREAD = 12.0
@@ -155,6 +157,7 @@
     ocn_vec_ref,
     vec_ref,
     weight_ref,
+    coeff_ref,
     small_sems,
     atm_sems,
     ocn_sems,
@@ -170,8 +173,10 @@
         load.start()
     atm_copies = tile_copies(atm_hbm, atm_ref, atm_sems)
     ocn_copies = tile_copies(ocn_hbm, ocn_ref, ocn_sems)
-    for copy in atm_copies + ocn_copies:
-        copy.start()
+    copies = [atm_copies, ocn_copies]
+    for region in REGIONS[:2]:
+        for which, t in region:
+            copies[which][t].start()
     even = lax.rem(lax.axis_index("tile"), 2) == 0
     lane = lax.broadcasted_iota(jnp.int32, (members, columns), 1)
 
@@ -206,25 +211,26 @@
                 total = jnp.where(lane == second + first + j, part[:, columns:], total)
         return total
 
-    def store(t, which, value):
-        lower = t < tiles // 2
-        slot = t if lower else t - tiles // 2
-
-        @pl.when(jnp.logical_not(even) if lower else even)
-        def _():
-            inner_ref[slot, which] = value
-
-        @pl.when(even if lower else jnp.logical_not(even))
-        def _():
-            outer_ref[slot, which] = value
-
-    for t in range(tiles):
-        atm_copies[t].wait()
-        store(t, 0, coefficients(atm_ref, t, t, atm_levels))
-    for t in range(tiles):
-        ocn_copies[t].wait()
-        sea = sea_ref[t].astype(F32)
-        store(t, 1, coefficients(ocn_ref, t, tiles + t, ocn_levels) * sea)
+    parts = [
+        (atm_ref, atm_copies, atm_levels),
+        (ocn_ref, ocn_copies, ocn_levels),
+    ]
+    for number, region in enumerate(REGIONS):
+        for which, t in region:
+            parts[which][1][t].wait()
+        for later in REGIONS[number + 2 : number + 2 + 1]:
+            for which, t in later:
+                copies[which][t].start()
+        for which, t in region:
+            ref, _, levels = parts[which]
+            total = coefficients(ref, t, which * tiles + t, levels)
+            if which == 1:
+                total = total * sea_ref[t].astype(F32)
+            coeff_ref[t, which] = total
+    half = tiles // 2
+    low, high = coeff_ref[:half], coeff_ref[half:]
+    inner_ref[...] = jnp.where(even, high, low)
+    outer_ref[...] = jnp.where(even, low, high)
 
 
 def second_kernel(
@@ -235,27 +241,24 @@
     outer_ref,
     inner_recv_ref,
     outer_recv_ref,
-    atm_cross_ref,
-    ocn_cross_ref,
+    atm_pair_ref,
+    ocn_pair_ref,
+    ocn_ref,
     atm_hbm,
-    ocn_hbm,
     atm_out_hbm,
     ocn_out_hbm,
     atm_ref,
-    ocn_ref,
     atm_out_ref,
     ocn_out_ref,
     padded_ref,
     vert_ref,
     out_sems,
     atm_sems,
-    ocn_sems,
 ):
     tiles, atm_levels, members, columns = atm_hbm.shape
-    ocn_levels = ocn_hbm.shape[1]
+    ocn_levels = ocn_ref.shape[1]
     atm_copies = tile_copies(atm_hbm, atm_ref, atm_sems)
-    ocn_copies = tile_copies(ocn_hbm, ocn_ref, ocn_sems)
-    for copy in atm_copies + ocn_copies:
+    for copy in atm_copies:
         copy.start()
     even = lax.rem(lax.axis_index("tile"), 2) == 0
     quarter = tiles // 2
@@ -290,10 +293,12 @@
         pltpu.make_async_copy(ocn_out_ref, ocn_out_hbm, out_sems.at[1]),
     ]
     parts = [
-        (atm_ref, atm_copies, atm_out_ref, atm_class_ref, atm_levels, ATM_SPREAD),
-        (ocn_ref, ocn_copies, ocn_out_ref, ocn_class_ref, ocn_levels, OCN_SPREAD),
-    ]
-    for which, (_, _, _, class_ref, _, width) in enumerate(parts):
+        (atm_ref, atm_out_ref, atm_pair_ref, atm_class_ref, atm_levels, ATM_SPREAD),
+        (ocn_ref, ocn_out_ref, ocn_pair_ref, ocn_class_ref, ocn_levels, OCN_SPREAD),
+    ]
+
+    def weights(which):
+        _, _, _, class_ref, _, width = parts[which]
         tapering = taper(width)
         for t in range(tiles):
             spread = jnp.zeros((members, columns), F32)
@@ -303,78 +308,71 @@
                 tapering, spread, NT, precision=lax.Precision.HIGHEST, preferred_element_type=F32
             ).astype(BF16)
 
-    for which, (ref, copies, out_ref, _, levels, _) in enumerate(parts):
-        for t in range(tiles):
-            copies[t].wait()
-            for start in range(0, levels, group):
-                count = min(group, levels - start)
-                right = jnp.concatenate([ref[t, start + j] for j in range(count)], axis=1)
-                product = jnp.dot(
-                    vert_ref[which, t, start : start + group, :], right, preferred_element_type=F32
-                )
-                total = product[:, :columns]
-                for j in range(1, count):
-                    total = jnp.where(sub == j, product[:, j * columns : (j + 1) * columns], total)
-                if which == 1:
-                    total = total * sea_ref[t].astype(F32)
-                out_ref[start : start + count, t, :] = total[:count]
-        if which == 0:
-            surface = levels - KA
-            out_ref[surface:] = out_ref[surface:] + atm_cross_ref[...]
-        else:
-            out_ref[:KO] = out_ref[:KO] + ocn_cross_ref[...]
+    def apply(which, t):
+        ref, out_ref, pair_ref, _, levels, _ = parts[which]
+        surface = [(levels - KA + i, RISE[i]) for i in range(KA)] if which == 0 else list(enumerate(FALL))
+        coupling = dict(surface)
+        paired = pair_ref[:, t * columns : (t + 1) * columns]
+        for start in range(0, levels, group):
+            count = min(group, levels - start)
+            right = jnp.concatenate([ref[t, start + j] for j in range(count)], axis=1)
+            product = jnp.dot(
+                vert_ref[which, t, start : start + group, :], right, preferred_element_type=F32
+            )
+            total = product[:, :columns]
+            for j in range(1, count):
+                total = jnp.where(sub == j, product[:, j * columns : (j + 1) * columns], total)
+            for j in range(count):
+                if start + j in coupling:
+                    term = jnp.sum(ref[t, start + j].astype(F32) * paired, axis=0, keepdims=True)
+                    term = term * (COUPLING * coupling[start + j])
+                    total = total + jnp.where(sub == j, term, 0.0)
+            if which == 1:
+                total = total * sea_ref[t].astype(F32)
+            out_ref[start : start + count, t, :] = total[:count]
+
+    def finish(which):
         stores[which].start()
+
+    weights(1)
+    weights(0)
+    for t in range(tiles):
+        apply(1, t)
+    finish(1)
+    for region in ATM_REGIONS:
+        for t in region:
+            atm_copies[t].wait()
+        for t in region:
+            apply(0, t)
+    finish(0)
     for store in stores:
         store.wait()
 
 
-def cross_kernel(
+def pair_kernel(
     per_peer,
-    sea_ref,
     pairing_ref,
     recv_ref,
-    atm_hbm,
     ocn_hbm,
-    atm_cross_ref,
-    ocn_cross_ref,
-    atm_top,
-    ocn_top,
+    atm_pair_ref,
+    ocn_pair_ref,
+    ocn_ref,
     sems,
 ):
-    tiles, atm_levels, members, columns = atm_hbm.shape
-    start = atm_levels - KA
-    loads = [
-        [
-            pltpu.make_async_copy(atm_hbm.at[t, pl.ds(start, KA)], atm_top.at[t], sems.at[0, t]),
-            pltpu.make_async_copy(ocn_hbm.at[t, pl.ds(0, KO)], ocn_top.at[t], sems.at[1, t]),
-        ]
-        for t in range(tiles)
-    ]
-    for pair in loads:
-        for load in pair:
-            load.start()
+    tiles, _, members, columns = ocn_hbm.shape
+    ocn_copies = tile_copies(ocn_hbm, ocn_ref, sems)
+    for copy in ocn_copies:
+        copy.start()
     peers, count = recv_ref.shape[0], recv_ref.shape[1] // 2
 
     def pair_columns(first, slots):
         rows = recv_ref[:, first : first + count, :].reshape(peers * count, members)
         return lax.dot_general(rows, slots, TN, preferred_element_type=F32)
 
-    atm_pair = pair_columns(count, atm_slots(pairing_ref, columns, tiles, per_peer))
-    ocn_pair = pair_columns(0, ocn_slots(columns, tiles, per_peer))
-
-    def rows_of(top, t, paired, weights):
-        part = paired[:, t * columns : (t + 1) * columns]
-        sums = [
-            jnp.sum(top[t, s].astype(F32) * part, axis=0, keepdims=True) * (COUPLING * weight)
-            for s, weight in enumerate(weights)
-        ]
-        return jnp.concatenate(sums, axis=0)
-
-    for t in range(tiles):
-        for load in loads[t]:
-            load.wait()
-        atm_cross_ref[:, t, :] = rows_of(atm_top, t, atm_pair, RISE)
-        ocn_cross_ref[:, t, :] = rows_of(ocn_top, t, ocn_pair, FALL) * sea_ref[t].astype(F32)
+    atm_pair_ref[...] = pair_columns(count, atm_slots(pairing_ref, columns, tiles, per_peer))
+    ocn_pair_ref[...] = pair_columns(0, ocn_slots(columns, tiles, per_peer))
+    for copy in ocn_copies:
+        copy.wait()
 
 
 def local(atm_anom, ocn_anom, atm_vec, ocn_vec, atm_to_ocean, sea_tiles, atm_class, ocn_class):
@@ -437,6 +435,7 @@
             pltpu.VMEM(ocn_rows.shape, BF16),
             pltpu.VMEM((2 * tiles, columns, columns), F32),
             pltpu.VMEM((2 * tiles, 2 * columns, 2 * columns), BF16),
+            pltpu.VMEM((tiles, 2, members, columns), F32),
             pltpu.SemaphoreType.DMA((3,)),
         ]
         + whole_sems,
@@ -450,19 +449,17 @@
     outer_recv = lax.ppermute(outer, "tile", outer_pairs)
     inner_recv = lax.ppermute(inner, "tile", [(i, i ^ 1) for i in range(count)])
 
-    atm_cross, ocn_cross = pl.pallas_call(
-        functools.partial(cross_kernel, per_peer),
-        out_shape=[
-            pltpu.VMEM((KA, tiles, columns), F32),
-            pltpu.VMEM((KO, tiles, columns), F32),
-        ],
-        in_specs=[SMEM_SPEC, VMEM_SPEC, VMEM_SPEC] + [ANY_SPEC] * 2,
-        out_specs=[VMEM_SPEC] * 2,
-        scratch_shapes=tops,
-        compiler_params=params,
+    pair = pltpu.VMEM((members, tiles * columns), F32)
+    atm_pair, ocn_pair, ocn_v = pl.pallas_call(
+        functools.partial(pair_kernel, per_peer),
+        out_shape=[pair, pair, pltpu.VMEM(ocn.shape, BF16)],
+        in_specs=[VMEM_SPEC, VMEM_SPEC, ANY_SPEC],
+        out_specs=[VMEM_SPEC] * 3,
+        scratch_shapes=[pltpu.SemaphoreType.DMA((tiles,))],
+        compiler_params=pltpu.CompilerParams(vmem_limit_bytes=54 * MIB),
         cost_estimate=cost(40 * top_elements, 4 * top_elements),
-        name="surface_cross",
-    )(sea_tiles, atm_to_ocean, in_vmem(incoming), atm, ocn)
+        name="pair_columns",
+    )(atm_to_ocean, in_vmem(incoming), ocn)
 
     atm_out, ocn_out = pl.pallas_call(
         second_kernel,
@@ -470,18 +467,18 @@
             jax.ShapeDtypeStruct((atm_levels, tiles, columns), F32),
             jax.ShapeDtypeStruct((ocn_levels, tiles, columns), F32),
         ],
-        in_specs=[SMEM_SPEC] * 3 + [VMEM_SPEC] * 6 + [ANY_SPEC] * 2,
+        in_specs=[SMEM_SPEC] * 3 + [VMEM_SPEC] * 7 + [ANY_SPEC],
         out_specs=[ANY_SPEC] * 2,
-        scratch_shapes=wholes
-        + [
+        scratch_shapes=[
+            pltpu.VMEM(atm.shape, BF16),
             pltpu.VMEM((atm_levels, tiles, columns), F32),
             pltpu.VMEM((ocn_levels, tiles, columns), F32),
             pltpu.VMEM((2 * tiles, 2, members, columns), F32),
             pltpu.VMEM((2, tiles, columns, members), BF16),
             pltpu.SemaphoreType.DMA((2,)),
-        ]
-        + whole_sems,
-        compiler_params=params,
+            pltpu.SemaphoreType.DMA((tiles,)),
+        ],
+        compiler_params=pltpu.CompilerParams(vmem_limit_bytes=50 * MIB),
         cost_estimate=cost(2 * 256 * elements, elements),
         name="second_pass",
     )(
@@ -492,10 +489,10 @@
         in_vmem(outer),
         in_vmem(inner_recv),
         in_vmem(outer_recv),
-        in_vmem(atm_cross),
-        in_vmem(ocn_cross),
+        in_vmem(atm_pair),
+        in_vmem(ocn_pair),
+        in_vmem(ocn_v),
         atm,
-        ocn,
     )
     return jnp.transpose(atm_out, (1, 0, 2)), jnp.transpose(ocn_out, (1, 0, 2))
 

time: 38.3 us -> 33.6 us (0.88)
  Pallas kernels: 24.8 us -> 21 us
  waiting for transfers between devices: 1.43 us -> 0.51 us
    pallas_call x1, Pallas kernels: 8.63 us -> 6.08 us  [local(): pl.pallas_call(second_kernel, out_shape=[jax.ShapeDtypeStruct((atm_levels...]
    pallas_call x1, Pallas kernels: 10.2 us -> 8.02 us  [local(): pl.pallas_call(first_kernel, out_shape=[edge, edge], in_specs=[ANY_SPEC]...]
    ppermute x1, waiting for transfers between devices: 1.43 us -> 0.5 us  [local(): outer_recv = lax.ppermute(outer, 'tile', outer_pairs)]
    pallas_call x1, Pallas kernels: 2.66 us -> 3.57 us  [local(): pl.pallas_call(functools.partial(pair_kernel, per_peer), out_shape=[pair,...]
  transfers between devices with their start and end apart: 3 -> 3, of which waited for: 1 -> 1; matrix products, arithmetic and copies ran while one was open for 0% -> 0% of each run, Pallas kernels for 34% -> 35%
where the time goes in v3:
time: 33.6 us; the launch traced here: 33.3 us
  Pallas kernels  21 us (62%)
  starting transfers between devices  11.1 us (33%)
  between operations  0.67 us (2%)
  waiting for transfers between devices  0.51 us (2%)
    pallas_call x1, Pallas kernels, local(): pl.pallas_call(first_kernel, out_shape=[edge, edge], in_specs=[ANY_SPEC]...  8.02 us
    all_to_all x1, starting transfers between devices, local(): lax.all_to_all(outgoing, axes, split_axis=0, concat_axis=0, tiled=True)  7.3 us
    pallas_call x1, Pallas kernels, local(): pl.pallas_call(second_kernel, out_shape=[jax.ShapeDtypeStruct((atm_levels...  6.08 us
    pallas_call x1, Pallas kernels, local(): pl.pallas_call(functools.partial(pair_kernel, per_peer), out_shape=[pair,...  3.57 us
    ppermute x1, starting transfers between devices, local(): outer_recv = lax.ppermute(outer, 'tile', outer_pairs)  3.48 us
    pallas_call x1, Pallas kernels, local(): pl.pallas_call(functools.partial(project_kernel, per_peer), out_shape=plt...  3.36 us
  transfers between devices with their start and end apart: 3, of which 1 were waited for; matrix products, arithmetic and copies ran while one was open for 0% of the time, Pallas kernels for 35%

profile of v3, /device:TPU:0, one launch (start us, length us, event | category | flops | bytes accessed | tf_op | source)
XLA Modules:
  0.0 33.3 jit_solution(4453163721506087246)
XLA Ops:
  0.6 3.4 %project.1 = bf16[32,32,80]{2,1,0:T(8,128)(2,1)} custom-call(s32[4]{0:T(128)} %sea_ref.1, s32[4,128]{1,0:T(4,128)} %pairing_ref.1, bf16[127,4,128]{2,1,0:T(4,128)(2,1)} %bitcast.12, bf16[75,4,128]{2,1,0:T(4,128)(2,1)} %bitcast.14, bf16[4,127,80,128]{3,2,1,0:T(8,128)(2,1)} %bitcast.6, bf16[4,75,80,128]{3,2,1,0:T(8,128)(2,1)} %bitcast.9), custom_call_target="tpu_custom_call" | custom-call | flops 5242880 | bytes 2621440 | tf_op jit(solution)/shard_map/project/pallas_call | solution.py:406
  4.0 7.3 %all-to-all-start = ((bf16[32,32,80]{2,1,0:T(8,128)(2,1)}), bf16[32,32,80]{2,1,0:T(8,128)(2,1)S(1)}, u32[]{:S(2)}, u32[]{:S(2)}) async-start(bf16[32,32,80]{2,1,0:T(8,128)(2,1)} %project.1), calls=%async_computation | async-start | bytes 524288 | tf_op jit(solution)/shard_map/all_to_all | solution.py:423
  11.3 8.0 %first_pass.1 = (f32[2,2,80,128]{3,2,1,0:T(8,128)S(1)}, f32[2,2,80,128]{3,2,1,0:T(8,128)S(1)}) custom-call(s32[4]{0:T(128)} %sea_ref.1, bf16[127,4,128]{2,1,0:T(4,128)(2,1)} %bitcast.13, bf16[75,4,128]{2,1,0:T(4,128)(2,1)} %bitcast.15, bf16[4,127,80,128]{3,2,1,0:T(8,128)(2,1)} %bitcast.7, bf16[4,75,80,128]{3,2,1,0:T(8,128)(2,1)} %bitcast.10), custom_call_target="tpu_custom_call" | custom-call | flops 4236247040 | bytes 16547840 | tf_op jit(solution)/shard_map/first_pass/pallas_call | solution.py:426
  19.3 0.3 collective-permute-start
  19.7 3.5 %collective-permute-start.1 = (f32[2,2,80,128]{3,2,1,0:T(8,128)S(1)}, f32[2,2,80,128]{3,2,1,0:T(8,128)S(1)}, u32[]{:S(2)}, u32[]{:S(2)}) collective-permute-start(f32[2,2,80,128]{3,2,1,0:T(8,128)S(1)} %get-tuple-element.10.outer_ref), channel_id=1, source_target_pairs={{0,7},{1,2},{2,1},{3,4},{4,3},{5,6},{6,5},{7,0},{8,15},{9,10},{10,... | collective-permute-start | bytes 491528 | tf_op jit(solution)/shard_map/ppermute | solution.py:449
  23.1 0.0 all-to-all-done.recv_ref
  23.1 3.6 %pair_columns.1 = (f32[80,512]{1,0:T(8,128)S(1)}, f32[80,512]{1,0:T(8,128)S(1)}, bf16[4,75,80,128]{3,2,1,0:T(8,128)(2,1)S(1)}) custom-call(s32[4,128]{1,0:T(4,128)} %pairing_ref.1, bf16[32,32,80]{2,1,0:T(8,128)(2,1)S(1)} %all-to-all-done.recv_ref, bf16[4,75,80,128]{3,2,1,0:T(8,128)(2,1)} %bitcast.11), custom_call_target="tpu_custom_call" | custom-call | flops 52428800 | bytes 10485760 | tf_op jit(solution)/shard_map/pair_columns/pallas_call | solution.py:453
  26.7 0.0 collective-permute-done.inner_recv_ref
  26.7 0.5 %collective-permute-done.1.outer_recv_ref = f32[2,2,80,128]{3,2,1,0:T(8,128)S(1)} collective-permute-done((f32[2,2,80,128]{3,2,1,0:T(8,128)S(1)}, f32[2,2,80,128]{3,2,1,0:T(8,128)S(1)}, u32[]{:S(2)}, u32[]{:S(2)}) %collective-permute-start.1) | collective-permute-done | bytes 163872 | tf_op jit(solution)/shard_map/ppermute | solution.py:449
  27.2 6.1 %second_pass.1 = (f32[127,4,128]{2,1,0:T(4,128)}, f32[75,4,128]{2,1,0:T(4,128)}) custom-call(s32[4]{0:T(128)} %sea_ref.1, s32[4,5]{1,0:T(4,128)} %atm_class_ref.1, s32[4,5]{1,0:T(4,128)} %ocn_class_ref.1, f32[2,2,80,128]{3,2,1,0:T(8,128)S(1)} %get-tuple-element.9.inner_ref, f32[2,2,80,128]{3,2,1,0:T(8,128)S(1)} %get-tuple-element.10.outer_ref, ...), custom_call_target="tpu_custom_call" | custom-call | flops 4236247040 | bytes 16547840 | tf_op jit(solution)/shard_map/second_pass/pallas_call | solution.py:464
Async XLA Ops:
  4.0 19.1 %all-to-all-start = ((bf16[32,32,80]{2,1,0:T(8,128)(2,1)}), bf16[32,32,80]{2,1,0:T(8,128)(2,1)S(1)}, u32[]{:S(2)}, u32[]{:S(2)}) async-start(bf16[32,32,80]{2,1,0:T(8,128)(2,1)} %project.1), calls=%async_computation | async-start | bytes 524288 | tf_op jit(solution)/shard_map/all_to_all | solution.py:423
  19.3 7.4 %collective-permute-start = (f32[2,2,80,128]{3,2,1,0:T(8,128)S(1)}, f32[2,2,80,128]{3,2,1,0:T(8,128)S(1)}, u32[]{:S(2)}, u32[]{:S(2)}) collective-permute-start(f32[2,2,80,128]{3,2,1,0:T(8,128)S(1)} %get-tuple-element.9.inner_ref), channel_id=1, source_target_pairs={{0,1},{1,0},{2,3},{3,2},{4,5},{5,4},{6,7},{7,6},{8,9},{9,8},{10,11... | collective-permute-start | bytes 491528 | tf_op jit(solution)/shard_map/ppermute | solution.py:450
  19.7 7.6 %collective-permute-start.1 = (f32[2,2,80,128]{3,2,1,0:T(8,128)S(1)}, f32[2,2,80,128]{3,2,1,0:T(8,128)S(1)}, u32[]{:S(2)}, u32[]{:S(2)}) collective-permute-start(f32[2,2,80,128]{3,2,1,0:T(8,128)S(1)} %get-tuple-element.10.outer_ref), channel_id=1, source_target_pairs={{0,7},{1,2},{2,1},{3,4},{4,3},{5,6},{6,5},{7,0},{8,15},{9,10},{10,... | collective-permute-start | bytes 491528 | tf_op jit(solution)/shard_map/ppermute | solution.py:449

commit v4 on v3

--- a/solution.py
+++ b/solution.py
@@ -11,8 +11,8 @@
 KA = 16
 KO = 16
 HALO = 2
-GROUP = 8
-ATM_REGIONS = [[0], [1], [2], [3]]
+GROUP = 4
+VECTOR_LEVELS = (31, 19)
 REGIONS = [[(0, 0)], [(0, 1), (0, 2)], [(0, 3), (1, 0)], [(1, 1), (1, 2), (1, 3)]]
 
 COUPLING = 8.0
@@ -59,10 +59,16 @@
     return pltpu.with_memory_space_constraint(array, pltpu.VMEM)
 
 
-def tile_copies(source, target, sems):
+def tile_copies(source, targets, sems):
+    first = source.shape[0] - len(targets)
     return [
-        pltpu.make_async_copy(source.at[t], target.at[t], sems.at[t]) for t in range(source.shape[0])
-    ]
+        pltpu.make_async_copy(source.at[first + i], target, sems.at[i])
+        for i, target in enumerate(targets)
+    ]
+
+
+def each(ref):
+    return [ref.at[i] for i in range(ref.shape[0])]
 
 
 def spread_vectors(source, vec_ref, which, tiles):
@@ -83,6 +89,8 @@
     atm_hbm,
     ocn_hbm,
     send_ref,
+    tile_ref,
+    tile_vec_ref,
     atm_top,
     ocn_top,
     sems,
@@ -97,15 +105,16 @@
     peers, count = send_ref.shape[0], send_ref.shape[1] // 2
     small = [
         pltpu.make_async_copy(pairing_hbm, pairing_ref, small_sems.at[0]),
-        pltpu.make_async_copy(atm_vec_hbm.at[pl.ds(start, KA)], atm_vec_ref, small_sems.at[1]),
+        pltpu.make_async_copy(atm_vec_hbm, atm_vec_ref, small_sems.at[1]),
         pltpu.make_async_copy(ocn_vec_hbm.at[pl.ds(0, KO)], ocn_vec_ref, small_sems.at[2]),
         pltpu.make_async_copy(sea_hbm, sea_ref, small_sems.at[3]),
     ]
     for load in small:
         load.start()
+    atm_tops = [tile_ref.at[pl.ds(start, KA)]] + [atm_top.at[t] for t in range(tiles - 1)]
     loads = [
         [
-            pltpu.make_async_copy(atm_hbm.at[t, pl.ds(start, KA)], atm_top.at[t], sems.at[0, t]),
+            pltpu.make_async_copy(atm_hbm.at[t, pl.ds(start, KA)], atm_tops[t], sems.at[0, t]),
             pltpu.make_async_copy(ocn_hbm.at[t, pl.ds(0, KO)], ocn_top.at[t], sems.at[1, t]),
         ]
         for t in range(tiles)
@@ -113,39 +122,49 @@
     for pair in loads:
         for load in pair:
             load.start()
+    rest = pltpu.make_async_copy(
+        atm_hbm.at[0, pl.ds(0, start)], tile_ref.at[pl.ds(0, start)], small_sems.at[4]
+    )
+    rest.start()
     for load in small:
         load.wait()
     slots = [
         atm_slots(pairing_ref, columns, tiles, per_peer),
         ocn_slots(columns, tiles, per_peer),
     ]
-    atm_rows = atm_vec_ref[...].astype(F32)
+    atm_rows = atm_vec_ref[start : start + KA].astype(F32)
     ocn_rows = ocn_vec_ref[...].astype(F32)
+    tile_vec_ref[:atm_levels] = atm_vec_ref[:, 0, :].astype(F32)
+    if atm_levels < columns:
+        tile_vec_ref[atm_levels:] = jnp.zeros((columns - atm_levels, columns), F32)
 
     def projection(top, t, rows, weights):
         total = jnp.zeros((members, columns), F32)
         for s, weight in enumerate(weights):
-            total = total + top[t, s].astype(F32) * (rows[s, t : t + 1, :] * weight)
+            total = total + top[s].astype(F32) * (rows[s, t : t + 1, :] * weight)
         return total
 
     atm_proj, ocn_proj = [], []
     for t in range(tiles):
         for load in loads[t]:
             load.wait()
-        atm_proj.append(projection(atm_top, t, atm_rows, RISE).astype(BF16))
+        atm_proj.append(projection(atm_tops[t], t, atm_rows, RISE).astype(BF16))
         sea = sea_ref[t].astype(F32)
-        ocn_proj.append((projection(ocn_top, t, ocn_rows, FALL) * sea).astype(BF16))
+        ocn_proj.append((projection(ocn_top.at[t], t, ocn_rows, FALL) * sea).astype(BF16))
     for place, proj in enumerate([atm_proj, ocn_proj]):
         rows = lax.dot_general(
             slots[place], jnp.concatenate(proj, axis=1), NT, preferred_element_type=F32
         ).astype(BF16)
         send_ref[:, place * count : (place + 1) * count, :] = rows.reshape(peers, count, members)
+    rest.wait()
 
 
 def first_kernel(
     sea_hbm,
     atm_vec_hbm,
     ocn_vec_hbm,
+    tile_ref,
+    tile_vec_ref,
     atm_hbm,
     ocn_hbm,
     inner_ref,
@@ -171,35 +190,35 @@
     ]
     for load in small:
         load.start()
-    atm_copies = tile_copies(atm_hbm, atm_ref, atm_sems)
-    ocn_copies = tile_copies(ocn_hbm, ocn_ref, ocn_sems)
-    copies = [atm_copies, ocn_copies]
-    for region in REGIONS[:2]:
+    atm_copies = tile_copies(atm_hbm, each(atm_ref), atm_sems)
+    ocn_copies = tile_copies(ocn_hbm, each(ocn_ref), ocn_sems)
+    copies = [[None] + atm_copies, ocn_copies]
+    held = [[tile_ref] + each(atm_ref), each(ocn_ref)]
+    for region in REGIONS[1:3]:
         for which, t in region:
             copies[which][t].start()
     even = lax.rem(lax.axis_index("tile"), 2) == 0
     lane = lax.broadcasted_iota(jnp.int32, (members, columns), 1)
 
     zeros = jnp.zeros((columns, columns), BF16)
-    for load in small:
-        load.wait()
-    spread_vectors(atm_vec_ref, vec_ref, 0, tiles)
-    spread_vectors(ocn_vec_ref, vec_ref, 1, tiles)
-    for place in range(2 * tiles):
+
+    def transpose_vectors(place):
         vec_t = vec_ref[place].T.astype(BF16)
         weight_ref[place, :columns, :columns] = vec_t
         weight_ref[place, :columns, columns:] = zeros
         weight_ref[place, columns:, :columns] = zeros
         weight_ref[place, columns:, columns:] = vec_t
 
-    def coefficients(ref, t, place, levels):
+    def coefficients(ref, place, levels):
+        vector_levels = VECTOR_LEVELS[place // tiles]
+        levels = levels - vector_levels
         half = (levels + 1) // 2
         second = levels - half
         total = jnp.zeros((members, columns), F32)
         for first in range(0, half, GROUP):
             count = min(GROUP, half - first)
-            left = ref[t, first : first + count].reshape(count * members, columns)
-            right = ref[t, second + first : second + first + count].reshape(count * members, columns)
+            left = ref[first : first + count].reshape(count * members, columns)
+            right = ref[second + first : second + first + count].reshape(count * members, columns)
             product = jnp.dot(
                 jnp.concatenate([left, right], axis=1),
                 weight_ref[place],
@@ -209,21 +228,30 @@
                 part = product[j * members : (j + 1) * members]
                 total = jnp.where(lane == first + j, part[:, :columns], total)
                 total = jnp.where(lane == second + first + j, part[:, columns:], total)
+        for level in range(levels, levels + vector_levels):
+            product = ref[level].astype(F32) * vec_ref[place, level : level + 1, :]
+            total = jnp.where(lane == level, jnp.sum(product, axis=1, keepdims=True), total)
         return total
 
-    parts = [
-        (atm_ref, atm_copies, atm_levels),
-        (ocn_ref, ocn_copies, ocn_levels),
-    ]
+    level_counts = [atm_levels, ocn_levels]
+    vec_ref[0] = tile_vec_ref[...]
+    transpose_vectors(0)
     for number, region in enumerate(REGIONS):
+        if number == 1:
+            for load in small:
+                load.wait()
+            spread_vectors(atm_vec_ref, vec_ref, 0, tiles)
+            spread_vectors(ocn_vec_ref, vec_ref, 1, tiles)
+            for place in range(1, 2 * tiles):
+                transpose_vectors(place)
         for which, t in region:
-            parts[which][1][t].wait()
-        for later in REGIONS[number + 2 : number + 2 + 1]:
+            if copies[which][t] is not None:
+                copies[which][t].wait()
+        for later in REGIONS[max(number + 2, 3) : number + 3]:
             for which, t in later:
                 copies[which][t].start()
         for which, t in region:
-            ref, _, levels = parts[which]
-            total = coefficients(ref, t, which * tiles + t, levels)
+            total = coefficients(held[which][t], which * tiles + t, level_counts[which])
             if which == 1:
                 total = total * sea_ref[t].astype(F32)
             coeff_ref[t, which] = total
@@ -244,6 +272,7 @@
     atm_pair_ref,
     ocn_pair_ref,
     ocn_ref,
+    tile_ref,
     atm_hbm,
     atm_out_hbm,
     ocn_out_hbm,
@@ -252,12 +281,13 @@
     ocn_out_ref,
     padded_ref,
     vert_ref,
+    column_ref,
     out_sems,
     atm_sems,
 ):
     tiles, atm_levels, members, columns = atm_hbm.shape
     ocn_levels = ocn_ref.shape[1]
-    atm_copies = tile_copies(atm_hbm, atm_ref, atm_sems)
+    atm_copies = tile_copies(atm_hbm, each(atm_ref), atm_sems)
     for copy in atm_copies:
         copy.start()
     even = lax.rem(lax.axis_index("tile"), 2) == 0
@@ -293,8 +323,8 @@
         pltpu.make_async_copy(ocn_out_ref, ocn_out_hbm, out_sems.at[1]),
     ]
     parts = [
-        (atm_ref, atm_out_ref, atm_pair_ref, atm_class_ref, atm_levels, ATM_SPREAD),
-        (ocn_ref, ocn_out_ref, ocn_pair_ref, ocn_class_ref, ocn_levels, OCN_SPREAD),
+        ([tile_ref] + each(atm_ref), atm_out_ref, atm_pair_ref, atm_class_ref, atm_levels, ATM_SPREAD),
+        (each(ocn_ref), ocn_out_ref, ocn_pair_ref, ocn_class_ref, ocn_levels, OCN_SPREAD),
     ]
 
     def weights(which):
@@ -304,29 +334,39 @@
             spread = jnp.zeros((members, columns), F32)
             for offset in range(2 * HALO + 1):
                 spread = spread + class_weight(class_ref[t, offset]) * padded_ref[t + offset, which]
-            vert_ref[which, t] = lax.dot_general(
+            vert = lax.dot_general(
                 tapering, spread, NT, precision=lax.Precision.HIGHEST, preferred_element_type=F32
             ).astype(BF16)
+            vert_ref[which, t] = vert
+            column_ref[which, t] = vert.astype(F32).T
 
     def apply(which, t):
-        ref, out_ref, pair_ref, _, levels, _ = parts[which]
+        refs, out_ref, pair_ref, _, levels, _ = parts[which]
+        ref = refs[t]
         surface = [(levels - KA + i, RISE[i]) for i in range(KA)] if which == 0 else list(enumerate(FALL))
         coupling = dict(surface)
         paired = pair_ref[:, t * columns : (t + 1) * columns]
         for start in range(0, levels, group):
             count = min(group, levels - start)
-            right = jnp.concatenate([ref[t, start + j] for j in range(count)], axis=1)
-            product = jnp.dot(
-                vert_ref[which, t, start : start + group, :], right, preferred_element_type=F32
-            )
-            total = product[:, :columns]
-            for j in range(1, count):
-                total = jnp.where(sub == j, product[:, j * columns : (j + 1) * columns], total)
+            plain = [j for j in range(count) if start + j not in coupling]
+            total = jnp.zeros((group, columns), F32)
+            if plain:
+                right = jnp.concatenate([ref[start + j] for j in plain], axis=1)
+                product = jnp.dot(
+                    vert_ref[which, t, start : start + group, :], right, preferred_element_type=F32
+                )
+                for place, j in enumerate(plain):
+                    part = product[:, place * columns : (place + 1) * columns]
+                    total = part if place == 0 else jnp.where(sub == j, part, total)
             for j in range(count):
-                if start + j in coupling:
-                    term = jnp.sum(ref[t, start + j].astype(F32) * paired, axis=0, keepdims=True)
-                    term = term * (COUPLING * coupling[start + j])
-                    total = total + jnp.where(sub == j, term, 0.0)
+                level = start + j
+                if level in coupling:
+                    column = jnp.broadcast_to(
+                        column_ref[which, t, :, level : level + 1], (members, columns)
+                    )
+                    factor = column + paired * (COUPLING * coupling[level])
+                    term = jnp.sum(ref[level].astype(F32) * factor, axis=0, keepdims=True)
+                    total = jnp.where(sub == j, term, total)
             if which == 1:
                 total = total * sea_ref[t].astype(F32)
             out_ref[start : start + count, t, :] = total[:count]
@@ -339,11 +379,10 @@
     for t in range(tiles):
         apply(1, t)
     finish(1)
-    for region in ATM_REGIONS:
-        for t in region:
-            atm_copies[t].wait()
-        for t in region:
-            apply(0, t)
+    apply(0, 0)
+    for t in range(1, tiles):
+        atm_copies[t - 1].wait()
+        apply(0, t)
     finish(0)
     for store in stores:
         store.wait()
@@ -360,7 +399,7 @@
     sems,
 ):
     tiles, _, members, columns = ocn_hbm.shape
-    ocn_copies = tile_copies(ocn_hbm, ocn_ref, sems)
+    ocn_copies = tile_copies(ocn_hbm, each(ocn_ref), sems)
     for copy in ocn_copies:
         copy.start()
     peers, count = recv_ref.shape[0], recv_ref.shape[1] // 2
@@ -392,29 +431,34 @@
 
     elements = tiles * members * columns * (atm_levels + ocn_levels)
     top_elements = tiles * members * columns * (KA + KO)
+    rest_shape = (tiles - 1,) + atm.shape[1:]
     tops = [
-        pltpu.VMEM((tiles, KA, members, columns), BF16),
+        pltpu.VMEM((tiles - 1, KA, members, columns), BF16),
         pltpu.VMEM((tiles, KO, members, columns), BF16),
         pltpu.SemaphoreType.DMA((2, tiles)),
     ]
-    wholes = [pltpu.VMEM(atm.shape, BF16), pltpu.VMEM(ocn.shape, BF16)]
+    wholes = [pltpu.VMEM(rest_shape, BF16), pltpu.VMEM(ocn.shape, BF16)]
     whole_sems = [pltpu.SemaphoreType.DMA((tiles,)), pltpu.SemaphoreType.DMA((tiles,))]
 
     def cost(flops, count):
         return pl.CostEstimate(flops=flops, bytes_accessed=2 * count, transcendentals=0)
 
-    outgoing = pl.pallas_call(
+    outgoing, tile, tile_vec = pl.pallas_call(
         functools.partial(project_kernel, per_peer),
-        out_shape=pltpu.VMEM((devices, 2 * peer_rows, members), BF16),
+        out_shape=[
+            jax.ShapeDtypeStruct((devices, 2 * peer_rows, members), BF16),
+            pltpu.VMEM((atm_levels, members, columns), BF16),
+            pltpu.VMEM((columns, columns), F32),
+        ],
         in_specs=[ANY_SPEC] * 6,
-        out_specs=VMEM_SPEC,
+        out_specs=[VMEM_SPEC] * 3,
         scratch_shapes=tops
         + [
             pltpu.SMEM(sea_tiles.shape, jnp.int32),
             pltpu.VMEM(atm_to_ocean.shape, jnp.int32),
-            pltpu.VMEM((KA, tiles, columns), BF16),
+            pltpu.VMEM(atm_rows.shape, BF16),
             pltpu.VMEM((KO, tiles, columns), BF16),
-            pltpu.SemaphoreType.DMA((4,)),
+            pltpu.SemaphoreType.DMA((5,)),
         ],
         compiler_params=params,
         cost_estimate=cost(4 * top_elements, top_elements),
@@ -426,7 +470,7 @@
     inner, outer = pl.pallas_call(
         first_kernel,
         out_shape=[edge, edge],
-        in_specs=[ANY_SPEC] * 5,
+        in_specs=[ANY_SPEC] * 3 + [VMEM_SPEC] * 2 + [ANY_SPEC] * 2,
         out_specs=[VMEM_SPEC] * 2,
         scratch_shapes=wholes
         + [
@@ -442,7 +486,7 @@
         compiler_params=params,
         cost_estimate=cost(2 * 256 * elements, elements),
         name="first_pass",
-    )(sea_tiles, atm_rows, ocn_rows, atm, ocn)
+    )(sea_tiles, atm_rows, ocn_rows, in_vmem(tile), in_vmem(tile_vec), atm, ocn)
 
     count = lax.axis_size("tile")
     outer_pairs = [(i, (i + 1) % count if i % 2 else (i - 1) % count) for i in range(count)]
@@ -456,7 +500,7 @@
         in_specs=[VMEM_SPEC, VMEM_SPEC, ANY_SPEC],
         out_specs=[VMEM_SPEC] * 3,
         scratch_shapes=[pltpu.SemaphoreType.DMA((tiles,))],
-        compiler_params=pltpu.CompilerParams(vmem_limit_bytes=54 * MIB),
+        compiler_params=pltpu.CompilerParams(vmem_limit_bytes=52 * MIB),
         cost_estimate=cost(40 * top_elements, 4 * top_elements),
         name="pair_columns",
     )(atm_to_ocean, in_vmem(incoming), ocn)
@@ -467,14 +511,15 @@
             jax.ShapeDtypeStruct((atm_levels, tiles, columns), F32),
             jax.ShapeDtypeStruct((ocn_levels, tiles, columns), F32),
         ],
-        in_specs=[SMEM_SPEC] * 3 + [VMEM_SPEC] * 7 + [ANY_SPEC],
+        in_specs=[SMEM_SPEC] * 3 + [VMEM_SPEC] * 8 + [ANY_SPEC],
         out_specs=[ANY_SPEC] * 2,
         scratch_shapes=[
-            pltpu.VMEM(atm.shape, BF16),
+            pltpu.VMEM(rest_shape, BF16),
             pltpu.VMEM((atm_levels, tiles, columns), F32),
             pltpu.VMEM((ocn_levels, tiles, columns), F32),
             pltpu.VMEM((2 * tiles, 2, members, columns), F32),
             pltpu.VMEM((2, tiles, columns, members), BF16),
+            pltpu.VMEM((2, tiles, members, columns), F32),
             pltpu.SemaphoreType.DMA((2,)),
             pltpu.SemaphoreType.DMA((tiles,)),
         ],
@@ -492,6 +537,7 @@
         in_vmem(atm_pair),
         in_vmem(ocn_pair),
         in_vmem(ocn_v),
+        in_vmem(tile),
         atm,
     )
     return jnp.transpose(atm_out, (1, 0, 2)), jnp.transpose(ocn_out, (1, 0, 2))

time: 33.6 us -> 31.8 us (0.946)
  Pallas kernels: 21 us -> 19.2 us
    pallas_call x1, Pallas kernels: 8.02 us -> 6.68 us  [local(): pl.pallas_call(first_kernel, out_shape=[edge, edge], in_specs=[ANY_SPEC]...]
    pallas_call x1, Pallas kernels: 6.08 us -> 5.49 us  [local(): pl.pallas_call(second_kernel, out_shape=[jax.ShapeDtypeStruct((atm_levels...]
  transfers between devices with their start and end apart: 3 -> 3, of which waited for: 1 -> 1; matrix products, arithmetic and copies ran while one was open for 0% -> 0% of each run, Pallas kernels for 35% -> 33%
where the time goes in v4:
time: 31.8 us; the launch traced here: 31.5 us
  Pallas kernels  19.2 us (60%)
  starting transfers between devices  11.1 us (35%)
  between operations  0.67 us (2%)
  waiting for transfers between devices  0.61 us (2%)
    all_to_all x1, starting transfers between devices, local(): lax.all_to_all(outgoing, axes, split_axis=0, concat_axis=0, tiled=True)  7.3 us
    pallas_call x1, Pallas kernels, local(): pl.pallas_call(first_kernel, out_shape=[edge, edge], in_specs=[ANY_SPEC]...  6.68 us
    pallas_call x1, Pallas kernels, local(): pl.pallas_call(second_kernel, out_shape=[jax.ShapeDtypeStruct((atm_levels...  5.49 us
    pallas_call x1, Pallas kernels, local(): pl.pallas_call(functools.partial(pair_kernel, per_peer), out_shape=[pair,...  3.57 us
    ppermute x1, starting transfers between devices, local(): outer_recv = lax.ppermute(outer, 'tile', outer_pairs)  3.49 us
    pallas_call x1, Pallas kernels, local(): pl.pallas_call(functools.partial(project_kernel, per_peer), out_shape=[ja...  3.41 us
  transfers between devices with their start and end apart: 3, of which 1 were waited for; matrix products, arithmetic and copies ran while one was open for 0% of the time, Pallas kernels for 33%

profile of v4, /device:TPU:0, one launch (start us, length us, event | category | flops | bytes accessed | tf_op | source)
XLA Modules:
  0.0 31.5 jit_solution(11875315087696316746)
XLA Ops:
  0.6 3.4 %project.1 = (bf16[32,32,80]{2,1,0:T(8,128)(2,1)}, bf16[127,80,128]{2,1,0:T(8,128)(2,1)S(1)}, f32[128,128]{1,0:T(8,128)S(1)}) custom-call(s32[4]{0:T(128)} %sea_ref.1, s32[4,128]{1,0:T(4,128)} %pairing_ref.1, bf16[127,4,128]{2,1,0:T(4,128)(2,1)} %bitcast.12, bf16[75,4,128]{2,1,0:T(4,128)(2,1)} %bitcast.14, bf16[4,127,80,128]{3,2,1,0:T(8,128)(2,1)} %bitcast.6, ...), custom_call_target="tpu_custom_call" | custom-call | flops 5242880 | bytes 2621440 | tf_op jit(solution)/shard_map/project/pallas_call | solution.py:446
  4.0 7.3 %all-to-all-start = ((bf16[32,32,80]{2,1,0:T(8,128)(2,1)}), bf16[32,32,80]{2,1,0:T(8,128)(2,1)S(1)}, u32[]{:S(2)}, u32[]{:S(2)}) async-start(bf16[32,32,80]{2,1,0:T(8,128)(2,1)} %get-tuple-element.16), calls=%async_computation | async-start | bytes 524288 | tf_op jit(solution)/shard_map/all_to_all | solution.py:467
  11.4 6.7 %first_pass.1 = (f32[2,2,80,128]{3,2,1,0:T(8,128)S(1)}, f32[2,2,80,128]{3,2,1,0:T(8,128)S(1)}) custom-call(s32[4]{0:T(128)} %sea_ref.1, bf16[127,4,128]{2,1,0:T(4,128)(2,1)} %bitcast.13, bf16[75,4,128]{2,1,0:T(4,128)(2,1)} %bitcast.15, bf16[127,80,128]{2,1,0:T(8,128)(2,1)S(1)} %get-tuple-element.12.tile_ref, f32[128,128]{1,0:T(8,128)S(1)} %get-tuple-element.13.tile_vec_ref, ...), custom_call_target="tpu_custom_call" | custom-call | flops 4236247040 | bytes 16547840 | tf_op jit(solution)/shard_map/first_pass/pallas_call | solution.py:470
  18.0 0.3 collective-permute-start
  18.4 3.5 %collective-permute-start.1 = (f32[2,2,80,128]{3,2,1,0:T(8,128)S(1)}, f32[2,2,80,128]{3,2,1,0:T(8,128)}, u32[]{:S(2)}, u32[]{:S(2)}) collective-permute-start(f32[2,2,80,128]{3,2,1,0:T(8,128)S(1)} %get-tuple-element.15.outer_ref), channel_id=1, source_target_pairs={{0,7},{1,2},{2,1},{3,4},{4,3},{5,6},{6,5},{7,0},{8,15},{9,10},{10,... | collective-permute-start | bytes 491528 | tf_op jit(solution)/shard_map/ppermute | solution.py:493
  21.8 0.0 all-to-all-done.recv_ref
  21.8 3.6 %pair_columns.1 = (f32[80,512]{1,0:T(8,128)S(1)}, f32[80,512]{1,0:T(8,128)S(1)}, bf16[4,75,80,128]{3,2,1,0:T(8,128)(2,1)S(1)}) custom-call(s32[4,128]{1,0:T(4,128)} %pairing_ref.1, bf16[32,32,80]{2,1,0:T(8,128)(2,1)S(1)} %all-to-all-done.recv_ref, bf16[4,75,80,128]{3,2,1,0:T(8,128)(2,1)} %bitcast.11), custom_call_target="tpu_custom_call" | custom-call | flops 52428800 | bytes 10485760 | tf_op jit(solution)/shard_map/pair_columns/pallas_call | solution.py:497
  25.4 0.0 collective-permute-done.inner_recv_ref
  25.4 0.6 %collective-permute-done.1.outer_recv_ref = f32[2,2,80,128]{3,2,1,0:T(8,128)} collective-permute-done((f32[2,2,80,128]{3,2,1,0:T(8,128)S(1)}, f32[2,2,80,128]{3,2,1,0:T(8,128)}, u32[]{:S(2)}, u32[]{:S(2)}) %collective-permute-start.1) | collective-permute-done | bytes 163872 | tf_op jit(solution)/shard_map/ppermute | solution.py:493
  26.0 5.5 %second_pass.1 = (f32[127,4,128]{2,1,0:T(4,128)}, f32[75,4,128]{2,1,0:T(4,128)}) custom-call(s32[4]{0:T(128)} %sea_ref.1, s32[4,5]{1,0:T(4,128)} %atm_class_ref.1, s32[4,5]{1,0:T(4,128)} %ocn_class_ref.1, f32[2,2,80,128]{3,2,1,0:T(8,128)S(1)} %get-tuple-element.14.inner_ref, f32[2,2,80,128]{3,2,1,0:T(8,128)S(1)} %get-tuple-element.15.outer_ref, ...), custom_call_target="tpu_custom_call" | custom-call | flops 4236247040 | bytes 16547840 | tf_op jit(solution)/shard_map/second_pass/pallas_call | solution.py:508
Async XLA Ops:
  4.0 17.8 %all-to-all-start = ((bf16[32,32,80]{2,1,0:T(8,128)(2,1)}), bf16[32,32,80]{2,1,0:T(8,128)(2,1)S(1)}, u32[]{:S(2)}, u32[]{:S(2)}) async-start(bf16[32,32,80]{2,1,0:T(8,128)(2,1)} %get-tuple-element.16), calls=%async_computation | async-start | bytes 524288 | tf_op jit(solution)/shard_map/all_to_all | solution.py:467
  18.0 7.4 %collective-permute-start = (f32[2,2,80,128]{3,2,1,0:T(8,128)S(1)}, f32[2,2,80,128]{3,2,1,0:T(8,128)S(1)}, u32[]{:S(2)}, u32[]{:S(2)}) collective-permute-start(f32[2,2,80,128]{3,2,1,0:T(8,128)S(1)} %get-tuple-element.14.inner_ref), channel_id=1, source_target_pairs={{0,1},{1,0},{2,3},{3,2},{4,5},{5,4},{6,7},{7,6},{8,9},{9,8},{10,11... | collective-permute-start | bytes 491528 | tf_op jit(solution)/shard_map/ppermute | solution.py:494
  18.4 7.7 %collective-permute-start.1 = (f32[2,2,80,128]{3,2,1,0:T(8,128)S(1)}, f32[2,2,80,128]{3,2,1,0:T(8,128)}, u32[]{:S(2)}, u32[]{:S(2)}) collective-permute-start(f32[2,2,80,128]{3,2,1,0:T(8,128)S(1)} %get-tuple-element.15.outer_ref), channel_id=1, source_target_pairs={{0,7},{1,2},{2,1},{3,4},{4,3},{5,6},{6,5},{7,0},{8,15},{9,10},{10,... | collective-permute-start | bytes 491528 | tf_op jit(solution)/shard_map/ppermute | solution.py:493

commit v5 on v4

--- a/solution.py
+++ b/solution.py
@@ -273,6 +273,7 @@
     ocn_pair_ref,
     ocn_ref,
     tile_ref,
+    next_ref,
     atm_hbm,
     atm_out_hbm,
     ocn_out_hbm,
@@ -323,7 +324,7 @@
         pltpu.make_async_copy(ocn_out_ref, ocn_out_hbm, out_sems.at[1]),
     ]
     parts = [
-        ([tile_ref] + each(atm_ref), atm_out_ref, atm_pair_ref, atm_class_ref, atm_levels, ATM_SPREAD),
+        ([tile_ref, next_ref] + each(atm_ref), atm_out_ref, atm_pair_ref, atm_class_ref, atm_levels, ATM_SPREAD),
         (each(ocn_ref), ocn_out_ref, ocn_pair_ref, ocn_class_ref, ocn_levels, OCN_SPREAD),
     ]
 
@@ -380,8 +381,9 @@
         apply(1, t)
     finish(1)
     apply(0, 0)
-    for t in range(1, tiles):
-        atm_copies[t - 1].wait()
+    apply(0, 1)
+    for t in range(2, tiles):
+        atm_copies[t - 2].wait()
         apply(0, t)
     finish(0)
     for store in stores:
@@ -393,14 +395,17 @@
     pairing_ref,
     recv_ref,
     ocn_hbm,
+    atm_hbm,
     atm_pair_ref,
     ocn_pair_ref,
     ocn_ref,
+    next_ref,
     sems,
 ):
     tiles, _, members, columns = ocn_hbm.shape
-    ocn_copies = tile_copies(ocn_hbm, each(ocn_ref), sems)
-    for copy in ocn_copies:
+    copies = tile_copies(ocn_hbm, each(ocn_ref), sems)
+    copies.append(pltpu.make_async_copy(atm_hbm.at[1], next_ref, sems.at[tiles]))
+    for copy in copies:
         copy.start()
     peers, count = recv_ref.shape[0], recv_ref.shape[1] // 2
 
@@ -410,7 +415,7 @@
 
     atm_pair_ref[...] = pair_columns(count, atm_slots(pairing_ref, columns, tiles, per_peer))
     ocn_pair_ref[...] = pair_columns(0, ocn_slots(columns, tiles, per_peer))
-    for copy in ocn_copies:
+    for copy in copies:
         copy.wait()
 
 
@@ -494,16 +499,21 @@
     inner_recv = lax.ppermute(inner, "tile", [(i, i ^ 1) for i in range(count)])
 
     pair = pltpu.VMEM((members, tiles * columns), F32)
-    atm_pair, ocn_pair, ocn_v = pl.pallas_call(
+    atm_pair, ocn_pair, ocn_v, next_tile = pl.pallas_call(
         functools.partial(pair_kernel, per_peer),
-        out_shape=[pair, pair, pltpu.VMEM(ocn.shape, BF16)],
-        in_specs=[VMEM_SPEC, VMEM_SPEC, ANY_SPEC],
-        out_specs=[VMEM_SPEC] * 3,
-        scratch_shapes=[pltpu.SemaphoreType.DMA((tiles,))],
-        compiler_params=pltpu.CompilerParams(vmem_limit_bytes=52 * MIB),
+        out_shape=[
+            pair,
+            pair,
+            pltpu.VMEM(ocn.shape, BF16),
+            pltpu.VMEM((atm_levels, members, columns), BF16),
+        ],
+        in_specs=[VMEM_SPEC, VMEM_SPEC, ANY_SPEC, ANY_SPEC],
+        out_specs=[VMEM_SPEC] * 4,
+        scratch_shapes=[pltpu.SemaphoreType.DMA((tiles + 1,))],
+        compiler_params=pltpu.CompilerParams(vmem_limit_bytes=44 * MIB),
         cost_estimate=cost(40 * top_elements, 4 * top_elements),
         name="pair_columns",
-    )(atm_to_ocean, in_vmem(incoming), ocn)
+    )(atm_to_ocean, in_vmem(incoming), ocn, atm)
 
     atm_out, ocn_out = pl.pallas_call(
         second_kernel,
@@ -511,10 +521,10 @@
             jax.ShapeDtypeStruct((atm_levels, tiles, columns), F32),
             jax.ShapeDtypeStruct((ocn_levels, tiles, columns), F32),
         ],
-        in_specs=[SMEM_SPEC] * 3 + [VMEM_SPEC] * 8 + [ANY_SPEC],
+        in_specs=[SMEM_SPEC] * 3 + [VMEM_SPEC] * 9 + [ANY_SPEC],
         out_specs=[ANY_SPEC] * 2,
         scratch_shapes=[
-            pltpu.VMEM(rest_shape, BF16),
+            pltpu.VMEM((tiles - 2,) + atm.shape[1:], BF16),
             pltpu.VMEM((atm_levels, tiles, columns), F32),
             pltpu.VMEM((ocn_levels, tiles, columns), F32),
             pltpu.VMEM((2 * tiles, 2, members, columns), F32),
@@ -523,7 +533,7 @@
             pltpu.SemaphoreType.DMA((2,)),
             pltpu.SemaphoreType.DMA((tiles,)),
         ],
-        compiler_params=pltpu.CompilerParams(vmem_limit_bytes=50 * MIB),
+        compiler_params=pltpu.CompilerParams(vmem_limit_bytes=42 * MIB),
         cost_estimate=cost(2 * 256 * elements, elements),
         name="second_pass",
     )(
@@ -538,6 +548,7 @@
         in_vmem(ocn_pair),
         in_vmem(ocn_v),
         in_vmem(tile),
+        in_vmem(next_tile),
         atm,
     )
     return jnp.transpose(atm_out, (1, 0, 2)), jnp.transpose(ocn_out, (1, 0, 2))

time: 31.8 us -> 31.1 us (0.978)
  Pallas kernels: 19.2 us -> 18.6 us
    pallas_call x1, Pallas kernels: 5.49 us -> 4.78 us  [local(): pl.pallas_call(second_kernel, out_shape=[jax.ShapeDtypeStruct((atm_levels...]
  transfers between devices with their start and end apart: 3 -> 3, of which waited for: 1 -> 1; matrix products, arithmetic and copies ran while one was open for 0% -> 0% of each run, Pallas kernels for 33% -> 34%
where the time goes in v5:
time: 31.1 us; the launch traced here: 30.9 us
  Pallas kernels  18.6 us (60%)
  starting transfers between devices  11.1 us (36%)
  between operations  0.68 us (2%)
  waiting for transfers between devices  0.5 us (2%)
    all_to_all x1, starting transfers between devices, local(): lax.all_to_all(outgoing, axes, split_axis=0, concat_axis=0, tiled=True)  7.3 us
    pallas_call x1, Pallas kernels, local(): pl.pallas_call(first_kernel, out_shape=[edge, edge], in_specs=[ANY_SPEC]...  6.67 us
    pallas_call x1, Pallas kernels, local(): pl.pallas_call(second_kernel, out_shape=[jax.ShapeDtypeStruct((atm_levels...  4.78 us
    pallas_call x1, Pallas kernels, local(): pl.pallas_call(functools.partial(pair_kernel, per_peer), out_shape=[pair,...  3.7 us
    ppermute x1, starting transfers between devices, local(): outer_recv = lax.ppermute(outer, 'tile', outer_pairs)  3.48 us
    pallas_call x1, Pallas kernels, local(): pl.pallas_call(functools.partial(project_kernel, per_peer), out_shape=[ja...  3.41 us
  transfers between devices with their start and end apart: 3, of which 1 were waited for; matrix products, arithmetic and copies ran while one was open for 0% of the time, Pallas kernels for 34%

profile of v5, /device:TPU:0, one launch (start us, length us, event | category | flops | bytes accessed | tf_op | source)
XLA Modules:
  0.0 30.9 jit_solution(11242129217390147640)
XLA Ops:
  0.6 3.4 %project.1 = (bf16[32,32,80]{2,1,0:T(8,128)(2,1)}, bf16[127,80,128]{2,1,0:T(8,128)(2,1)S(1)}, f32[128,128]{1,0:T(8,128)S(1)}) custom-call(s32[4]{0:T(128)} %sea_ref.1, s32[4,128]{1,0:T(4,128)} %pairing_ref.1, bf16[127,4,128]{2,1,0:T(4,128)(2,1)} %bitcast.13, bf16[75,4,128]{2,1,0:T(4,128)(2,1)} %bitcast.15, bf16[4,127,80,128]{3,2,1,0:T(8,128)(2,1)} %bitcast.6, ...), custom_call_target="tpu_custom_call" | custom-call | flops 5242880 | bytes 2621440 | tf_op jit(solution)/shard_map/project/pallas_call | solution.py:451
  4.1 7.3 %all-to-all-start = ((bf16[32,32,80]{2,1,0:T(8,128)(2,1)}), bf16[32,32,80]{2,1,0:T(8,128)(2,1)S(1)}, u32[]{:S(2)}, u32[]{:S(2)}) async-start(bf16[32,32,80]{2,1,0:T(8,128)(2,1)} %get-tuple-element.17), calls=%async_computation | async-start | bytes 524288 | tf_op jit(solution)/shard_map/all_to_all | solution.py:472
  11.4 0.0 copy-start
  11.4 6.7 %first_pass.1 = (f32[2,2,80,128]{3,2,1,0:T(8,128)S(1)}, f32[2,2,80,128]{3,2,1,0:T(8,128)S(1)}) custom-call(s32[4]{0:T(128)} %sea_ref.1, bf16[127,4,128]{2,1,0:T(4,128)(2,1)} %bitcast.14, bf16[75,4,128]{2,1,0:T(4,128)(2,1)} %bitcast.16, bf16[127,80,128]{2,1,0:T(8,128)(2,1)S(1)} %get-tuple-element.13.tile_ref, f32[128,128]{1,0:T(8,128)S(1)} %get-tuple-element.14.tile_vec_ref, ...), custom_call_target="tpu_custom_call" | custom-call | flops 4236247040 | bytes 16547840 | tf_op jit(solution)/shard_map/first_pass/pallas_call | solution.py:475
  18.1 0.3 %collective-permute-start = (f32[2,2,80,128]{3,2,1,0:T(8,128)S(1)}, f32[2,2,80,128]{3,2,1,0:T(8,128)S(1)}, u32[]{:S(2)}, u32[]{:S(2)}) collective-permute-start(f32[2,2,80,128]{3,2,1,0:T(8,128)S(1)} %get-tuple-element.15.inner_ref), channel_id=1, source_target_pairs={{0,1},{1,0},{2,3},{3,2},{4,5},{5,4},{6,7},{7,6},{8,9},{9,8},{10,11... | collective-permute-start | bytes 491528 | tf_op jit(solution)/shard_map/ppermute | solution.py:499
  18.4 0.0 copy-start.1
  18.4 0.0 copy-start.2
  18.4 0.0 copy-start.3
  18.4 3.5 %collective-permute-start.1 = (f32[2,2,80,128]{3,2,1,0:T(8,128)S(1)}, f32[2,2,80,128]{3,2,1,0:T(8,128)}, u32[]{:S(2)}, u32[]{:S(2)}) collective-permute-start(f32[2,2,80,128]{3,2,1,0:T(8,128)S(1)} %get-tuple-element.16.outer_ref), channel_id=1, source_target_pairs={{0,7},{1,2},{2,1},{3,4},{4,3},{5,6},{6,5},{7,0},{8,15},{9,10},{10,... | collective-permute-start | bytes 491528 | tf_op jit(solution)/shard_map/ppermute | solution.py:498
  21.9 0.0 all-to-all-done.recv_ref
  21.9 0.0 copy-done
  21.9 3.7 %pair_columns.1 = (f32[80,512]{1,0:T(8,128)S(1)}, f32[80,512]{1,0:T(8,128)S(1)}, bf16[4,75,80,128]{3,2,1,0:T(8,128)(2,1)S(1)}, bf16[127,80,128]{2,1,0:T(8,128)(2,1)S(1)}) custom-call(s32[4,128]{1,0:T(4,128)S(1)} %copy-done, bf16[32,32,80]{2,1,0:T(8,128)(2,1)S(1)} %all-to-all-done.recv_ref, bf16[4,75,80,128]{3,2,1,0:T(8,128)(2,1)} %bitcast.12, ...), custom_call_target="tpu_custom_call" | custom-call | flops 52428800 | bytes 10485760 | tf_op jit(solution)/shard_map/pair_columns/pallas_call | solution.py:502
  25.6 0.0 collective-permute-done.inner_recv_ref
  25.6 0.5 %collective-permute-done.1.outer_recv_ref = f32[2,2,80,128]{3,2,1,0:T(8,128)} collective-permute-done((f32[2,2,80,128]{3,2,1,0:T(8,128)S(1)}, f32[2,2,80,128]{3,2,1,0:T(8,128)}, u32[]{:S(2)}, u32[]{:S(2)}) %collective-permute-start.1) | collective-permute-done | bytes 163872 | tf_op jit(solution)/shard_map/ppermute | solution.py:498
  26.1 0.0 copy-done.1
  26.1 0.0 copy-done.2
  26.1 0.0 copy-done.3
  26.1 4.8 %second_pass.1 = (f32[127,4,128]{2,1,0:T(4,128)}, f32[75,4,128]{2,1,0:T(4,128)}) custom-call(s32[4]{0:T(128)S(1)} %copy-done.1, s32[4,5]{1,0:T(4,128)S(1)} %copy-done.2, s32[4,5]{1,0:T(4,128)S(1)} %copy-done.3, f32[2,2,80,128]{3,2,1,0:T(8,128)S(1)} %get-tuple-element.15.inner_ref, f32[2,2,80,128]{3,2,1,0:T(8,128)S(1)} %get-tuple-element.16.outer_ref, ...), custom_call_target="tpu_custom_call" | custom-call | flops 4236247040 | bytes 16547840 | tf_op jit(solution)/shard_map/second_pass/pallas_call | solution.py:518
Async XLA Ops:
  4.1 17.8 %all-to-all-start = ((bf16[32,32,80]{2,1,0:T(8,128)(2,1)}), bf16[32,32,80]{2,1,0:T(8,128)(2,1)S(1)}, u32[]{:S(2)}, u32[]{:S(2)}) async-start(bf16[32,32,80]{2,1,0:T(8,128)(2,1)} %get-tuple-element.17), calls=%async_computation | async-start | bytes 524288 | tf_op jit(solution)/shard_map/all_to_all | solution.py:472
  11.4 10.5 %copy-start = (s32[4,128]{1,0:T(4,128)S(1)}, s32[4,128]{1,0:T(4,128)}, u32[]{:S(2)}) copy-start(s32[4,128]{1,0:T(4,128)} %pairing_ref.1) | copy-start | bytes 6148
  18.1 7.5 %collective-permute-start = (f32[2,2,80,128]{3,2,1,0:T(8,128)S(1)}, f32[2,2,80,128]{3,2,1,0:T(8,128)S(1)}, u32[]{:S(2)}, u32[]{:S(2)}) collective-permute-start(f32[2,2,80,128]{3,2,1,0:T(8,128)S(1)} %get-tuple-element.15.inner_ref), channel_id=1, source_target_pairs={{0,1},{1,0},{2,3},{3,2},{4,5},{5,4},{6,7},{7,6},{8,9},{9,8},{10,11... | collective-permute-start | bytes 491528 | tf_op jit(solution)/shard_map/ppermute | solution.py:499
  18.4 7.7 %copy-start.1 = (s32[4]{0:T(128)S(1)}, s32[4]{0:T(128)}, u32[]{:S(2)}) copy-start(s32[4]{0:T(128)} %sea_ref.1) | copy-start | bytes 52
  18.4 7.7 %copy-start.2 = (s32[4,5]{1,0:T(4,128)S(1)}, s32[4,5]{1,0:T(4,128)}, u32[]{:S(2)}) copy-start(s32[4,5]{1,0:T(4,128)} %atm_class_ref.1) | copy-start | bytes 244
  18.4 7.7 %copy-start.3 = (s32[4,5]{1,0:T(4,128)S(1)}, s32[4,5]{1,0:T(4,128)}, u32[]{:S(2)}) copy-start(s32[4,5]{1,0:T(4,128)} %ocn_class_ref.1) | copy-start | bytes 244
  18.4 7.7 %collective-permute-start.1 = (f32[2,2,80,128]{3,2,1,0:T(8,128)S(1)}, f32[2,2,80,128]{3,2,1,0:T(8,128)}, u32[]{:S(2)}, u32[]{:S(2)}) collective-permute-start(f32[2,2,80,128]{3,2,1,0:T(8,128)S(1)} %get-tuple-element.16.outer_ref), channel_id=1, source_target_pairs={{0,7},{1,2},{2,1},{3,4},{4,3},{5,6},{6,5},{7,0},{8,15},{9,10},{10,... | collective-permute-start | bytes 491528 | tf_op jit(solution)/shard_map/ppermute | solution.py:498

commit v6 on v5

--- a/solution.py
+++ b/solution.py
@@ -13,7 +13,7 @@
 HALO = 2
 GROUP = 4
 VECTOR_LEVELS = (31, 19)
-REGIONS = [[(0, 0)], [(0, 1), (0, 2)], [(0, 3), (1, 0)], [(1, 1), (1, 2), (1, 3)]]
+REGIONS = [[(0, 0)], [(0, 1)], [(0, 2), (0, 3)], [(1, 0), (1, 1)], [(1, 2), (1, 3)]]
 
 COUPLING = 8.0
 ATM_SPREAD = 12.0
@@ -119,19 +119,17 @@
         ]
         for t in range(tiles)
     ]
-    for pair in loads:
-        for load in pair:
-            load.start()
+    for place in range(2):
+        for pair in loads:
+            pair[place].start()
     rest = pltpu.make_async_copy(
         atm_hbm.at[0, pl.ds(0, start)], tile_ref.at[pl.ds(0, start)], small_sems.at[4]
     )
     rest.start()
+    slots = [None, ocn_slots(columns, tiles, per_peer)]
     for load in small:
         load.wait()
-    slots = [
-        atm_slots(pairing_ref, columns, tiles, per_peer),
-        ocn_slots(columns, tiles, per_peer),
-    ]
+    slots[0] = atm_slots(pairing_ref, columns, tiles, per_peer)
     atm_rows = atm_vec_ref[start : start + KA].astype(F32)
     ocn_rows = ocn_vec_ref[...].astype(F32)
     tile_vec_ref[:atm_levels] = atm_vec_ref[:, 0, :].astype(F32)
@@ -144,18 +142,25 @@
             total = total + top[s].astype(F32) * (rows[s, t : t + 1, :] * weight)
         return total
 
-    atm_proj, ocn_proj = [], []
-    for t in range(tiles):
-        for load in loads[t]:
-            load.wait()
-        atm_proj.append(projection(atm_tops[t], t, atm_rows, RISE).astype(BF16))
-        sea = sea_ref[t].astype(F32)
-        ocn_proj.append((projection(ocn_top.at[t], t, ocn_rows, FALL) * sea).astype(BF16))
-    for place, proj in enumerate([atm_proj, ocn_proj]):
+    def route(place, proj):
         rows = lax.dot_general(
             slots[place], jnp.concatenate(proj, axis=1), NT, preferred_element_type=F32
         ).astype(BF16)
         send_ref[:, place * count : (place + 1) * count, :] = rows.reshape(peers, count, members)
+
+    for t in range(tiles):
+        loads[t][0].wait()
+    atm_proj = [
+        projection(atm_tops[t], t, atm_rows, RISE).astype(BF16) for t in range(tiles)
+    ]
+    for t in range(tiles):
+        loads[t][1].wait()
+    route(0, atm_proj)
+    ocn_proj = [
+        (projection(ocn_top.at[t], t, ocn_rows, FALL) * sea_ref[t].astype(F32)).astype(BF16)
+        for t in range(tiles)
+    ]
+    route(1, ocn_proj)
     rest.wait()
 
 
@@ -496,7 +501,8 @@
     count = lax.axis_size("tile")
     outer_pairs = [(i, (i + 1) % count if i % 2 else (i - 1) % count) for i in range(count)]
     outer_recv = lax.ppermute(outer, "tile", outer_pairs)
-    inner_recv = lax.ppermute(inner, "tile", [(i, i ^ 1) for i in range(count)])
+    sent, incoming = lax.optimization_barrier((inner, incoming))
+    inner_recv = lax.ppermute(sent, "tile", [(i, i ^ 1) for i in range(count)])
 
     pair = pltpu.VMEM((members, tiles * columns), F32)
     atm_pair, ocn_pair, ocn_v, next_tile = pl.pallas_call(

time: 31.1 us -> 30.5 us (0.981)
  Pallas kernels: 18.6 us -> 18.1 us
    ppermute x1, waiting for transfers between devices: 0.49 us -> 0.01 us  [local(): outer_recv = lax.ppermute(outer, 'tile', outer_pairs)]
    pallas_call x1, Pallas kernels: 4.78 us -> 4.45 us  [local(): pl.pallas_call(second_kernel, out_shape=[jax.ShapeDtypeStruct((atm_levels...]
where the time goes in v6:
time: 30.5 us; the launch traced here: 30.3 us
  Pallas kernels  18.1 us (59%)
  starting transfers between devices  11.1 us (36%)
  between operations  0.71 us (2%)
    all_to_all x1, starting transfers between devices, local(): lax.all_to_all(outgoing, axes, split_axis=0, concat_axis=0, tiled=True)  7.3 us
    pallas_call x1, Pallas kernels, local(): pl.pallas_call(first_kernel, out_shape=[edge, edge], in_specs=[ANY_SPEC]...  6.63 us
    pallas_call x1, Pallas kernels, local(): pl.pallas_call(second_kernel, out_shape=[jax.ShapeDtypeStruct((atm_levels...  4.45 us
    pallas_call x1, Pallas kernels, local(): pl.pallas_call(functools.partial(pair_kernel, per_peer), out_shape=[pair,...  3.69 us
    ppermute x1, starting transfers between devices, local(): outer_recv = lax.ppermute(outer, 'tile', outer_pairs)  3.44 us
    pallas_call x1, Pallas kernels, local(): pl.pallas_call(functools.partial(project_kernel, per_peer), out_shape=[ja...  3.35 us
  transfers between devices with their start and end apart: 3, of which 1 were waited for; matrix products, arithmetic and copies ran while one was open for 0% of the time, Pallas kernels for 34%

profile of v6, /device:TPU:0, one launch (start us, length us, event | category | flops | bytes accessed | tf_op | source)
XLA Modules:
  0.0 30.3 jit_solution(9702447683061322786)
XLA Ops:
  0.6 3.4 %project.1 = (bf16[32,32,80]{2,1,0:T(8,128)(2,1)}, bf16[127,80,128]{2,1,0:T(8,128)(2,1)S(1)}, f32[128,128]{1,0:T(8,128)S(1)}) custom-call(s32[4]{0:T(128)} %sea_ref.1, s32[4,128]{1,0:T(4,128)} %pairing_ref.1, bf16[127,4,128]{2,1,0:T(4,128)(2,1)} %bitcast.13, bf16[75,4,128]{2,1,0:T(4,128)(2,1)} %bitcast.15, bf16[4,127,80,128]{3,2,1,0:T(8,128)(2,1)} %bitcast.6, ...), custom_call_target="tpu_custom_call" | custom-call | flops 5242880 | bytes 2621440 | tf_op jit(solution)/shard_map/project/pallas_call | solution.py:456
  4.0 7.3 %all-to-all-start = ((bf16[32,32,80]{2,1,0:T(8,128)(2,1)}), bf16[32,32,80]{2,1,0:T(8,128)(2,1)S(1)}, u32[]{:S(2)}, u32[]{:S(2)}) async-start(bf16[32,32,80]{2,1,0:T(8,128)(2,1)} %get-tuple-element.19), calls=%async_computation | async-start | bytes 524288 | tf_op jit(solution)/shard_map/all_to_all | solution.py:477
  11.3 0.0 copy-start
  11.3 6.6 %first_pass.1 = (f32[2,2,80,128]{3,2,1,0:T(8,128)S(1)}, f32[2,2,80,128]{3,2,1,0:T(8,128)S(1)}) custom-call(s32[4]{0:T(128)} %sea_ref.1, bf16[127,4,128]{2,1,0:T(4,128)(2,1)} %bitcast.14, bf16[75,4,128]{2,1,0:T(4,128)(2,1)} %bitcast.16, bf16[127,80,128]{2,1,0:T(8,128)(2,1)S(1)} %get-tuple-element.15.tile_ref, f32[128,128]{1,0:T(8,128)S(1)} %get-tuple-element.16.tile_vec_ref, ...), custom_call_target="tpu_custom_call" | custom-call | flops 4236247040 | bytes 16547840 | tf_op jit(solution)/shard_map/first_pass/pallas_call | solution.py:480
  17.9 3.4 %collective-permute-start.1 = (f32[2,2,80,128]{3,2,1,0:T(8,128)S(1)}, f32[2,2,80,128]{3,2,1,0:T(8,128)S(1)}, u32[]{:S(2)}, u32[]{:S(2)}) collective-permute-start(f32[2,2,80,128]{3,2,1,0:T(8,128)S(1)} %get-tuple-element.18.outer_ref), channel_id=1, source_target_pairs={{0,7},{1,2},{2,1},{3,4},{4,3},{5,6},{6,5},{7,0},{8,15},{9,10},{10,... | collective-permute-start | bytes 491528 | tf_op jit(solution)/shard_map/ppermute | solution.py:503
  21.4 0.3 all-to-all-done.recv_ref
  21.7 0.0 copy-start.1
  21.7 0.0 copy-start.2
  21.7 0.0 copy-start.3
  21.7 0.4 %collective-permute-start = (f32[2,2,80,128]{3,2,1,0:T(8,128)S(1)}, f32[2,2,80,128]{3,2,1,0:T(8,128)S(1)}, u32[]{:S(2)}, u32[]{:S(2)}) collective-permute-start(f32[2,2,80,128]{3,2,1,0:T(8,128)S(1)} %get-tuple-element.20.inner_ref), channel_id=1, source_target_pairs={{0,1},{1,0},{2,3},{3,2},{4,5},{5,4},{6,7},{7,6},{8,9},{9,8},{10,11... | collective-permute-start | bytes 491528 | tf_op jit(solution)/shard_map/ppermute | solution.py:505
  22.1 0.0 copy-done
  22.1 3.7 %pair_columns.1 = (f32[80,512]{1,0:T(8,128)S(1)}, f32[80,512]{1,0:T(8,128)S(1)}, bf16[4,75,80,128]{3,2,1,0:T(8,128)(2,1)S(1)}, bf16[127,80,128]{2,1,0:T(8,128)(2,1)S(1)}) custom-call(s32[4,128]{1,0:T(4,128)S(1)} %copy-done, bf16[32,32,80]{2,1,0:T(8,128)(2,1)S(1)} %all-to-all-done.recv_ref, bf16[4,75,80,128]{3,2,1,0:T(8,128)(2,1)} %bitcast.12, ...), custom_call_target="tpu_custom_call" | custom-call | flops 52428800 | bytes 10485760 | tf_op jit(solution)/shard_map/pair_columns/pallas_call | solution.py:508
  25.8 0.0 collective-permute-done.1.outer_recv_ref
  25.8 0.0 collective-permute-done.inner_recv_ref
  25.8 0.0 copy-done.1
  25.8 0.0 copy-done.2
  25.8 0.0 copy-done.3
  25.8 4.4 %second_pass.1 = (f32[127,4,128]{2,1,0:T(4,128)}, f32[75,4,128]{2,1,0:T(4,128)}) custom-call(s32[4]{0:T(128)S(1)} %copy-done.1, s32[4,5]{1,0:T(4,128)S(1)} %copy-done.2, s32[4,5]{1,0:T(4,128)S(1)} %copy-done.3, f32[2,2,80,128]{3,2,1,0:T(8,128)S(1)} %get-tuple-element.20.inner_ref, f32[2,2,80,128]{3,2,1,0:T(8,128)S(1)} %get-tuple-element.18.outer_ref, ...), custom_call_target="tpu_custom_call" | custom-call | flops 4236247040 | bytes 16547840 | tf_op jit(solution)/shard_map/second_pass/pallas_call | solution.py:524
Async XLA Ops:
  4.0 17.7 %all-to-all-start = ((bf16[32,32,80]{2,1,0:T(8,128)(2,1)}), bf16[32,32,80]{2,1,0:T(8,128)(2,1)S(1)}, u32[]{:S(2)}, u32[]{:S(2)}) async-start(bf16[32,32,80]{2,1,0:T(8,128)(2,1)} %get-tuple-element.19), calls=%async_computation | async-start | bytes 524288 | tf_op jit(solution)/shard_map/all_to_all | solution.py:477
  11.3 10.8 %copy-start = (s32[4,128]{1,0:T(4,128)S(1)}, s32[4,128]{1,0:T(4,128)}, u32[]{:S(2)}) copy-start(s32[4,128]{1,0:T(4,128)} %pairing_ref.1) | copy-start | bytes 6148
  17.9 7.8 %collective-permute-start.1 = (f32[2,2,80,128]{3,2,1,0:T(8,128)S(1)}, f32[2,2,80,128]{3,2,1,0:T(8,128)S(1)}, u32[]{:S(2)}, u32[]{:S(2)}) collective-permute-start(f32[2,2,80,128]{3,2,1,0:T(8,128)S(1)} %get-tuple-element.18.outer_ref), channel_id=1, source_target_pairs={{0,7},{1,2},{2,1},{3,4},{4,3},{5,6},{6,5},{7,0},{8,15},{9,10},{10,... | collective-permute-start | bytes 491528 | tf_op jit(solution)/shard_map/ppermute | solution.py:503
  21.7 4.1 %copy-start.1 = (s32[4]{0:T(128)S(1)}, s32[4]{0:T(128)}, u32[]{:S(2)}) copy-start(s32[4]{0:T(128)} %sea_ref.1) | copy-start | bytes 52
  21.7 4.1 %copy-start.2 = (s32[4,5]{1,0:T(4,128)S(1)}, s32[4,5]{1,0:T(4,128)}, u32[]{:S(2)}) copy-start(s32[4,5]{1,0:T(4,128)} %atm_class_ref.1) | copy-start | bytes 244
  21.7 4.1 %copy-start.3 = (s32[4,5]{1,0:T(4,128)S(1)}, s32[4,5]{1,0:T(4,128)}, u32[]{:S(2)}) copy-start(s32[4,5]{1,0:T(4,128)} %ocn_class_ref.1) | copy-start | bytes 244
  21.7 4.1 %collective-permute-start = (f32[2,2,80,128]{3,2,1,0:T(8,128)S(1)}, f32[2,2,80,128]{3,2,1,0:T(8,128)S(1)}, u32[]{:S(2)}, u32[]{:S(2)}) collective-permute-start(f32[2,2,80,128]{3,2,1,0:T(8,128)S(1)} %get-tuple-element.20.inner_ref), channel_id=1, source_target_pairs={{0,1},{1,0},{2,3},{3,2},{4,5},{5,4},{6,7},{7,6},{8,9},{9,8},{10,11... | collective-permute-start | bytes 491528 | tf_op jit(solution)/shard_map/ppermute | solution.py:505

commit v7 on v6

--- a/solution.py
+++ b/solution.py
@@ -71,13 +71,16 @@
     return [ref.at[i] for i in range(ref.shape[0])]
 
 
-def spread_vectors(source, vec_ref, which, tiles):
-    levels, _, columns = source.shape
+def whole_rows(levels):
+    return -(-levels // 16) * 16
+
+
+def spread_vectors(source, levels, vec_ref, which, tiles):
+    columns = source.shape[2]
     for t in range(tiles):
         place = which * tiles + t
-        vec_ref[place, :levels] = source[:, t, :].astype(F32)
-        if levels < columns:
-            vec_ref[place, levels:] = jnp.zeros((columns - levels, columns), F32)
+        vec_ref[place] = jnp.zeros((columns, columns), F32)
+        vec_ref[place, :levels] = source[:levels, t, :].astype(F32)
 
 
 def project_kernel(
@@ -105,7 +108,9 @@
     peers, count = send_ref.shape[0], send_ref.shape[1] // 2
     small = [
         pltpu.make_async_copy(pairing_hbm, pairing_ref, small_sems.at[0]),
-        pltpu.make_async_copy(atm_vec_hbm, atm_vec_ref, small_sems.at[1]),
+        pltpu.make_async_copy(
+            atm_vec_hbm, atm_vec_ref.at[pl.ds(0, atm_levels)], small_sems.at[1]
+        ),
         pltpu.make_async_copy(ocn_vec_hbm.at[pl.ds(0, KO)], ocn_vec_ref, small_sems.at[2]),
         pltpu.make_async_copy(sea_hbm, sea_ref, small_sems.at[3]),
     ]
@@ -132,9 +137,8 @@
     slots[0] = atm_slots(pairing_ref, columns, tiles, per_peer)
     atm_rows = atm_vec_ref[start : start + KA].astype(F32)
     ocn_rows = ocn_vec_ref[...].astype(F32)
-    tile_vec_ref[:atm_levels] = atm_vec_ref[:, 0, :].astype(F32)
-    if atm_levels < columns:
-        tile_vec_ref[atm_levels:] = jnp.zeros((columns - atm_levels, columns), F32)
+    tile_vec_ref[...] = jnp.zeros((columns, columns), F32)
+    tile_vec_ref[:atm_levels] = atm_vec_ref[:atm_levels, 0, :].astype(F32)
 
     def projection(top, t, rows, weights):
         total = jnp.zeros((members, columns), F32)
@@ -189,8 +193,12 @@
     tiles, atm_levels, members, columns = atm_hbm.shape
     ocn_levels = ocn_hbm.shape[1]
     small = [
-        pltpu.make_async_copy(atm_vec_hbm, atm_vec_ref, small_sems.at[0]),
-        pltpu.make_async_copy(ocn_vec_hbm, ocn_vec_ref, small_sems.at[1]),
+        pltpu.make_async_copy(
+            atm_vec_hbm, atm_vec_ref.at[pl.ds(0, atm_levels)], small_sems.at[0]
+        ),
+        pltpu.make_async_copy(
+            ocn_vec_hbm, ocn_vec_ref.at[pl.ds(0, ocn_levels)], small_sems.at[1]
+        ),
         pltpu.make_async_copy(sea_hbm, sea_ref, small_sems.at[2]),
     ]
     for load in small:
@@ -245,8 +253,8 @@
         if number == 1:
             for load in small:
                 load.wait()
-            spread_vectors(atm_vec_ref, vec_ref, 0, tiles)
-            spread_vectors(ocn_vec_ref, vec_ref, 1, tiles)
+            spread_vectors(atm_vec_ref, atm_levels, vec_ref, 0, tiles)
+            spread_vectors(ocn_vec_ref, ocn_levels, vec_ref, 1, tiles)
             for place in range(1, 2 * tiles):
                 transpose_vectors(place)
         for which, t in region:
@@ -325,8 +333,12 @@
         return jnp.exp(-0.5 * scaled * scaled)
 
     stores = [
-        pltpu.make_async_copy(atm_out_ref, atm_out_hbm, out_sems.at[0]),
-        pltpu.make_async_copy(ocn_out_ref, ocn_out_hbm, out_sems.at[1]),
+        pltpu.make_async_copy(
+            atm_out_ref.at[pl.ds(0, atm_levels)], atm_out_hbm, out_sems.at[0]
+        ),
+        pltpu.make_async_copy(
+            ocn_out_ref.at[pl.ds(0, ocn_levels)], ocn_out_hbm, out_sems.at[1]
+        ),
     ]
     parts = [
         ([tile_ref, next_ref] + each(atm_ref), atm_out_ref, atm_pair_ref, atm_class_ref, atm_levels, ATM_SPREAD),
@@ -466,7 +478,7 @@
         + [
             pltpu.SMEM(sea_tiles.shape, jnp.int32),
             pltpu.VMEM(atm_to_ocean.shape, jnp.int32),
-            pltpu.VMEM(atm_rows.shape, BF16),
+            pltpu.VMEM((whole_rows(atm_levels), tiles, columns), BF16),
             pltpu.VMEM((KO, tiles, columns), BF16),
             pltpu.SemaphoreType.DMA((5,)),
         ],
@@ -485,8 +497,8 @@
         scratch_shapes=wholes
         + [
             pltpu.SMEM(sea_tiles.shape, jnp.int32),
-            pltpu.VMEM(atm_rows.shape, BF16),
-            pltpu.VMEM(ocn_rows.shape, BF16),
+            pltpu.VMEM((whole_rows(atm_levels), tiles, columns), BF16),
+            pltpu.VMEM((whole_rows(ocn_levels), tiles, columns), BF16),
             pltpu.VMEM((2 * tiles, columns, columns), F32),
             pltpu.VMEM((2 * tiles, 2 * columns, 2 * columns), BF16),
             pltpu.VMEM((tiles, 2, members, columns), F32),
@@ -531,8 +543,8 @@
         out_specs=[ANY_SPEC] * 2,
         scratch_shapes=[
             pltpu.VMEM((tiles - 2,) + atm.shape[1:], BF16),
-            pltpu.VMEM((atm_levels, tiles, columns), F32),
-            pltpu.VMEM((ocn_levels, tiles, columns), F32),
+            pltpu.VMEM((whole_rows(atm_levels), tiles, columns), F32),
+            pltpu.VMEM((whole_rows(ocn_levels), tiles, columns), F32),
             pltpu.VMEM((2 * tiles, 2, members, columns), F32),
             pltpu.VMEM((2, tiles, columns, members), BF16),
             pltpu.VMEM((2, tiles, members, columns), F32),

time: 30.5 us -> 30.5 us (level)
  no operation moved by 1% of the time
where the time goes in v7:
time: 30.5 us; the launch traced here: 30.3 us
  Pallas kernels  18.1 us (59%)
  starting transfers between devices  11.1 us (36%)
  between operations  0.71 us (2%)
    all_to_all x1, starting transfers between devices, local(): lax.all_to_all(outgoing, axes, split_axis=0, concat_axis=0, tiled=True)  7.3 us
    pallas_call x1, Pallas kernels, local(): pl.pallas_call(first_kernel, out_shape=[edge, edge], in_specs=[ANY_SPEC]...  6.64 us
    pallas_call x1, Pallas kernels, local(): pl.pallas_call(second_kernel, out_shape=[jax.ShapeDtypeStruct((atm_levels...  4.45 us
    pallas_call x1, Pallas kernels, local(): pl.pallas_call(functools.partial(pair_kernel, per_peer), out_shape=[pair,...  3.69 us
    ppermute x1, starting transfers between devices, local(): outer_recv = lax.ppermute(outer, 'tile', outer_pairs)  3.43 us
    pallas_call x1, Pallas kernels, local(): pl.pallas_call(functools.partial(project_kernel, per_peer), out_shape=[ja...  3.35 us
  transfers between devices with their start and end apart: 3, of which 1 were waited for; matrix products, arithmetic and copies ran while one was open for 0% of the time, Pallas kernels for 34%

profile of v7, /device:TPU:0, one launch (start us, length us, event | category | flops | bytes accessed | tf_op | source)
XLA Modules:
  0.0 30.3 jit_solution(6286552604525784338)
XLA Ops:
  0.6 3.4 %project.1 = (bf16[32,32,80]{2,1,0:T(8,128)(2,1)}, bf16[127,80,128]{2,1,0:T(8,128)(2,1)S(1)}, f32[128,128]{1,0:T(8,128)S(1)}) custom-call(s32[4]{0:T(128)} %sea_ref.1, s32[4,128]{1,0:T(4,128)} %pairing_ref.1, bf16[127,4,128]{2,1,0:T(4,128)(2,1)} %bitcast.13, bf16[75,4,128]{2,1,0:T(4,128)(2,1)} %bitcast.15, bf16[4,127,80,128]{3,2,1,0:T(8,128)(2,1)} %bitcast.6, ...), custom_call_target="tpu_custom_call" | custom-call | flops 5242880 | bytes 2621440 | tf_op jit(solution)/shard_map/project/pallas_call | solution.py:468
  4.0 7.3 %all-to-all-start = ((bf16[32,32,80]{2,1,0:T(8,128)(2,1)}), bf16[32,32,80]{2,1,0:T(8,128)(2,1)S(1)}, u32[]{:S(2)}, u32[]{:S(2)}) async-start(bf16[32,32,80]{2,1,0:T(8,128)(2,1)} %get-tuple-element.19), calls=%async_computation | async-start | bytes 524288 | tf_op jit(solution)/shard_map/all_to_all | solution.py:489
  11.3 0.0 copy-start
  11.3 6.6 %first_pass.1 = (f32[2,2,80,128]{3,2,1,0:T(8,128)S(1)}, f32[2,2,80,128]{3,2,1,0:T(8,128)S(1)}) custom-call(s32[4]{0:T(128)} %sea_ref.1, bf16[127,4,128]{2,1,0:T(4,128)(2,1)} %bitcast.14, bf16[75,4,128]{2,1,0:T(4,128)(2,1)} %bitcast.16, bf16[127,80,128]{2,1,0:T(8,128)(2,1)S(1)} %get-tuple-element.15.tile_ref, f32[128,128]{1,0:T(8,128)S(1)} %get-tuple-element.16.tile_vec_ref, ...), custom_call_target="tpu_custom_call" | custom-call | flops 4236247040 | bytes 16547840 | tf_op jit(solution)/shard_map/first_pass/pallas_call | solution.py:492
  18.0 3.4 %collective-permute-start.1 = (f32[2,2,80,128]{3,2,1,0:T(8,128)S(1)}, f32[2,2,80,128]{3,2,1,0:T(8,128)S(1)}, u32[]{:S(2)}, u32[]{:S(2)}) collective-permute-start(f32[2,2,80,128]{3,2,1,0:T(8,128)S(1)} %get-tuple-element.18.outer_ref), channel_id=1, source_target_pairs={{0,7},{1,2},{2,1},{3,4},{4,3},{5,6},{6,5},{7,0},{8,15},{9,10},{10,... | collective-permute-start | bytes 491528 | tf_op jit(solution)/shard_map/ppermute | solution.py:515
  21.4 0.3 all-to-all-done.recv_ref
  21.7 0.0 copy-start.1
  21.7 0.0 copy-start.2
  21.7 0.0 copy-start.3
  21.7 0.4 %collective-permute-start = (f32[2,2,80,128]{3,2,1,0:T(8,128)S(1)}, f32[2,2,80,128]{3,2,1,0:T(8,128)S(1)}, u32[]{:S(2)}, u32[]{:S(2)}) collective-permute-start(f32[2,2,80,128]{3,2,1,0:T(8,128)S(1)} %get-tuple-element.20.inner_ref), channel_id=1, source_target_pairs={{0,1},{1,0},{2,3},{3,2},{4,5},{5,4},{6,7},{7,6},{8,9},{9,8},{10,11... | collective-permute-start | bytes 491528 | tf_op jit(solution)/shard_map/ppermute | solution.py:517
  22.1 0.0 copy-done
  22.1 3.7 %pair_columns.1 = (f32[80,512]{1,0:T(8,128)S(1)}, f32[80,512]{1,0:T(8,128)S(1)}, bf16[4,75,80,128]{3,2,1,0:T(8,128)(2,1)S(1)}, bf16[127,80,128]{2,1,0:T(8,128)(2,1)S(1)}) custom-call(s32[4,128]{1,0:T(4,128)S(1)} %copy-done, bf16[32,32,80]{2,1,0:T(8,128)(2,1)S(1)} %all-to-all-done.recv_ref, bf16[4,75,80,128]{3,2,1,0:T(8,128)(2,1)} %bitcast.12, ...), custom_call_target="tpu_custom_call" | custom-call | flops 52428800 | bytes 10485760 | tf_op jit(solution)/shard_map/pair_columns/pallas_call | solution.py:520
  25.8 0.0 collective-permute-done.1.outer_recv_ref
  25.8 0.0 collective-permute-done.inner_recv_ref
  25.8 0.0 copy-done.1
  25.8 0.0 copy-done.2
  25.8 0.0 copy-done.3
  25.8 4.4 %second_pass.1 = (f32[127,4,128]{2,1,0:T(4,128)}, f32[75,4,128]{2,1,0:T(4,128)}) custom-call(s32[4]{0:T(128)S(1)} %copy-done.1, s32[4,5]{1,0:T(4,128)S(1)} %copy-done.2, s32[4,5]{1,0:T(4,128)S(1)} %copy-done.3, f32[2,2,80,128]{3,2,1,0:T(8,128)S(1)} %get-tuple-element.20.inner_ref, f32[2,2,80,128]{3,2,1,0:T(8,128)S(1)} %get-tuple-element.18.outer_ref, ...), custom_call_target="tpu_custom_call" | custom-call | flops 4236247040 | bytes 16547840 | tf_op jit(solution)/shard_map/second_pass/pallas_call | solution.py:536
Async XLA Ops:
  4.0 17.7 %all-to-all-start = ((bf16[32,32,80]{2,1,0:T(8,128)(2,1)}), bf16[32,32,80]{2,1,0:T(8,128)(2,1)S(1)}, u32[]{:S(2)}, u32[]{:S(2)}) async-start(bf16[32,32,80]{2,1,0:T(8,128)(2,1)} %get-tuple-element.19), calls=%async_computation | async-start | bytes 524288 | tf_op jit(solution)/shard_map/all_to_all | solution.py:489
  11.3 10.8 %copy-start = (s32[4,128]{1,0:T(4,128)S(1)}, s32[4,128]{1,0:T(4,128)}, u32[]{:S(2)}) copy-start(s32[4,128]{1,0:T(4,128)} %pairing_ref.1) | copy-start | bytes 6148
  18.0 7.8 %collective-permute-start.1 = (f32[2,2,80,128]{3,2,1,0:T(8,128)S(1)}, f32[2,2,80,128]{3,2,1,0:T(8,128)S(1)}, u32[]{:S(2)}, u32[]{:S(2)}) collective-permute-start(f32[2,2,80,128]{3,2,1,0:T(8,128)S(1)} %get-tuple-element.18.outer_ref), channel_id=1, source_target_pairs={{0,7},{1,2},{2,1},{3,4},{4,3},{5,6},{6,5},{7,0},{8,15},{9,10},{10,... | collective-permute-start | bytes 491528 | tf_op jit(solution)/shard_map/ppermute | solution.py:515
  21.7 4.1 %copy-start.1 = (s32[4]{0:T(128)S(1)}, s32[4]{0:T(128)}, u32[]{:S(2)}) copy-start(s32[4]{0:T(128)} %sea_ref.1) | copy-start | bytes 52
  21.7 4.1 %copy-start.2 = (s32[4,5]{1,0:T(4,128)S(1)}, s32[4,5]{1,0:T(4,128)}, u32[]{:S(2)}) copy-start(s32[4,5]{1,0:T(4,128)} %atm_class_ref.1) | copy-start | bytes 244
  21.7 4.1 %copy-start.3 = (s32[4,5]{1,0:T(4,128)S(1)}, s32[4,5]{1,0:T(4,128)}, u32[]{:S(2)}) copy-start(s32[4,5]{1,0:T(4,128)} %ocn_class_ref.1) | copy-start | bytes 244
  21.7 4.1 %collective-permute-start = (f32[2,2,80,128]{3,2,1,0:T(8,128)S(1)}, f32[2,2,80,128]{3,2,1,0:T(8,128)S(1)}, u32[]{:S(2)}, u32[]{:S(2)}) collective-permute-start(f32[2,2,80,128]{3,2,1,0:T(8,128)S(1)} %get-tuple-element.20.inner_ref), channel_id=1, source_target_pairs={{0,1},{1,0},{2,3},{3,2},{4,5},{5,4},{6,7},{7,6},{8,9},{9,8},{10,11... | collective-permute-start | bytes 491528 | tf_op jit(solution)/shard_map/ppermute | solution.py:517
